TPU v7x, 256 devices: a whole 4x4x8 slice. The times are simulated.
256 devices in a mesh: tm: 32 (over z, x_lo, core), tile: 8 (over y, x_hi).
Axes of the slice: x: 4 (x_hi: 2, x_lo: 2; x = x_hi * 2 + x_lo), y: 4, z: 8, core: 2. Of those that a mesh axis runs over, the one named last changes fastest.
Arguments:
- queries: bfloat16 [256, 192, 3072], P(('tm', 'tile')), may hold values from -120 to 120
- keys: bfloat16 [256, 192, 3072], P(('tm', 'tile')), may hold values from -4.6 to 4.6
- values: bfloat16 [256, 192, 3072], P(('tm', 'tile')), may hold values from -6 to 6
- grad_out: bfloat16 [256, 192, 3072], P(('tm', 'tile')), may hold values from -6 to 6
Outputs:
- grad_queries: bfloat16 [256, 192, 3072], P('tm', 'tile')
- grad_keys: bfloat16 [256, 192, 3072], P('tm', 'tile')
- grad_values: bfloat16 [256, 192, 3072], P('tm', 'tile')
All inputs are finite; a program needn't handle non-finite values.
Results may differ from a plain program's by a relative error of at most 0.011.
Values may be sent and summed in bfloat16 or wider, within the bound.
No kernel may reach another device: no remote copies, remote signals or barrier semaphores. Data moves between devices by JAX's collectives and lax.ppermute only.
A program may use at most 128 MiB of HBM per device.

v0:
```python
import math

import jax
import jax.numpy as jnp
from jax import lax
from jax.sharding import PartitionSpec as P

DH = 128


def shifted(block, axis, distance):
    devices = range(lax.axis_size(axis))
    route = [((i - distance) % len(devices), i) for i in devices]
    return lax.ppermute(block, axis, route)


def neighbour_slabs(own_keys, own_values):
    fetched = [(own_keys, own_values)]
    passing = (own_keys, own_values)
    for distance in range(3):
        passing = shifted((passing[0], passing[1]), "tm", 1)
        fetched.append(passing)
    return fetched


def shards(queries, keys, values, grad_out):
    slab_q, slab_k, slab_v, slab_g = (
        lax.all_to_all(queries, "tile", split_axis=1, concat_axis=0, tiled=True),
        lax.all_to_all(keys, "tile", split_axis=1, concat_axis=0, tiled=True),
        lax.all_to_all(values, "tile", split_axis=1, concat_axis=0, tiled=True),
        lax.all_to_all(grad_out, "tile", split_axis=1, concat_axis=0, tiled=True),
    )
    fetched = neighbour_slabs(slab_k, slab_v)
    frames, spatial, feature_count = slab_q.shape
    row_count = frames * spatial
    head_count = feature_count // DH
    group_heads = 8
    group_width = group_heads * DH
    group_total = head_count // group_heads
    scaling = 1.0 / math.sqrt(DH)
    flat_q = slab_q.reshape(row_count, feature_count)
    flat_g = slab_g.reshape(row_count, feature_count)
    all_keys = jnp.concatenate(
        [slab_pair[0].reshape(row_count, feature_count) for slab_pair in fetched], axis=0
    )
    all_values = jnp.concatenate(
        [slab_pair[1].reshape(row_count, feature_count) for slab_pair in fetched], axis=0
    )

    def cut(source, offset, rows):
        return lax.dynamic_slice_in_dim(source, offset, group_width, 1).reshape(
            rows, group_heads, DH
        )

    def window_pass(offset):
        query_cut = cut(flat_q, offset, row_count)
        grad_cut = cut(flat_g, offset, row_count)
        key_cut = cut(all_keys, offset, 4 * row_count)
        value_cut = cut(all_values, offset, 4 * row_count)
        scores = (
            jnp.einsum("qhd,khd->hqk", query_cut, key_cut, preferred_element_type=jnp.float32)
            * scaling
        )
        peak = jnp.max(scores, axis=-1, keepdims=True)
        log_total = peak + jnp.log(jnp.sum(jnp.exp(scores - peak), axis=-1, keepdims=True))
        weights = jnp.exp(scores - log_total)
        weights_low = weights.astype(jnp.bfloat16)
        output = jnp.einsum(
            "hqk,khd->qhd", weights_low, value_cut, preferred_element_type=jnp.float32
        )
        row_delta = jnp.sum(grad_cut.astype(jnp.float32) * output, axis=-1).T
        dprobs = jnp.einsum("qhd,khd->hqk", grad_cut, value_cut, preferred_element_type=jnp.float32)
        dscores = (weights * (dprobs - row_delta[:, :, None])).astype(jnp.bfloat16)
        part_q = (
            jnp.einsum("hqk,khd->qhd", dscores, key_cut, preferred_element_type=jnp.float32)
            * scaling
        )
        return (query_cut, grad_cut, log_total[:, :, 0], row_delta, weights_low, dscores, part_q)

    def one_group(group_index, totals):
        grad_q, grad_k, grad_v = totals
        offset = group_index * group_width
        query_cut, grad_cut, log_total, row_delta, weights_low, dscores, part_q = window_pass(
            offset
        )
        part_k = (
            jnp.einsum("hqk,qhd->khd", dscores, query_cut, preferred_element_type=jnp.float32)
            * scaling
        )
        part_v = jnp.einsum(
            "hqk,qhd->khd", weights_low, grad_cut, preferred_element_type=jnp.float32
        )
        grad_q = lax.dynamic_update_slice_in_dim(
            grad_q, part_q.reshape(row_count, group_width).astype(jnp.bfloat16), offset, 1
        )
        grad_k = lax.dynamic_update_slice_in_dim(
            grad_k, part_k.reshape(4 * row_count, group_width), offset, 1
        )
        grad_v = lax.dynamic_update_slice_in_dim(
            grad_v, part_v.reshape(4 * row_count, group_width), offset, 1
        )
        return (grad_q, grad_k, grad_v)

    start_totals = (
        jnp.zeros((row_count, feature_count), jnp.bfloat16),
        jnp.zeros((4 * row_count, feature_count), jnp.float32),
        jnp.zeros((4 * row_count, feature_count), jnp.float32),
    )
    grad_q, grad_k, grad_v = lax.fori_loop(0, group_total, one_group, start_totals)
    key_parts = grad_k.reshape(4, row_count, feature_count)
    value_parts = grad_v.reshape(4, row_count, feature_count)
    key_total = key_parts[0]
    value_total = value_parts[0]
    for distance in (1, 2, 3):
        back_keys, back_values = shifted(
            (key_parts[distance], value_parts[distance]), "tm", -distance
        )
        key_total = key_total + back_keys
        value_total = value_total + back_values
    return (
        grad_q.reshape(frames, spatial, feature_count),
        key_total.astype(jnp.bfloat16).reshape(frames, spatial, feature_count),
        value_total.astype(jnp.bfloat16).reshape(frames, spatial, feature_count),
    )


def solution(mesh):
    in_specs = (
        P(("tm", "tile"), None, None),
        P(("tm", "tile"), None, None),
        P(("tm", "tile"), None, None),
        P(("tm", "tile"), None, None),
    )
    out_specs = (P("tm", "tile", None), P("tm", "tile", None), P("tm", "tile", None))
    return jax.shard_map(shards, mesh=mesh, in_specs=in_specs, out_specs=out_specs, check_vma=False)
```

profile of v0, /device:TPU:33, one launch (start us, length us, event | category | flops | bytes accessed | tf_op | source)
XLA Modules:
  0.0 582.7 jit_solution(9778004344428847169)
XLA Ops:
  4.2 7.7 %reduce = bf16[192,3072]{1,0:T(8,128)(2,1)S(1)} reduce(bf16[192,1,3072]{2,1,0:T(2,128)(2,1)S(1)} %bitcast.132, bf16[]{:T(256)} %broadcast.39), dimensions={1}, to_apply=%bitcast.77.reduce_sub_computation | reduce | bytes 2359298
  13.5 6.9 %all-to-all-start = ((bf16[8,2,36864]{2,1,0:T(2,128)(2,1)}), bf16[8,2,36864]{2,1,0:T(2,128)(2,1)S(1)}, u32[]{:S(2)}, u32[]{:S(2)}) async-start(bf16[8,2,36864]{2,1,0:T(2,128)(2,1)} %reshape.156), calls=%async_computation | async-start | bytes 2359296 | tf_op jit(solution)/shard_map/all_to_all | solution.py:29
  23.5 8.7 %reduce.3 = bf16[192,3072]{1,0:T(8,128)(2,1)} reduce(bf16[192,1,3072]{2,1,0:T(2,128)(2,1)S(1)} %bitcast.134, bf16[]{:T(256)} %broadcast.39), dimensions={1}, to_apply=%bitcast.74.reduce_sub_computation | reduce | bytes 2359298
  38.1 4.3 all-to-all-start.3
  47.0 11.8 %all-to-all-done.3 = bf16[8,2,36864]{2,1,0:T(2,128)(2,1)} async-done(((bf16[8,2,36864]{2,1,0:T(2,128)(2,1)}), bf16[8,2,36864]{2,1,0:T(2,128)(2,1)}, u32[]{:S(2)}, u32[]{:S(2)}) %all-to-all-start.3) | async-done | bytes 1179680 | tf_op jit(solution)/shard_map/all_to_all | solution.py:30
  58.8 5.9 %reshape.163 = bf16[192,1,3072]{2,1,0:T(2,128)(2,1)} reshape(bf16[8,2,36864]{2,1,0:T(2,128)(2,1)} %all-to-all-done.3) | data formatting | bytes 2359296
  67.8 16.4 %collective-permute-start.3 = (bf16[8,24,3072]{2,1,0:T(8,128)(2,1)}, bf16[8,24,3072]{2,1,0:T(8,128)(2,1)}, u32[]{:S(2)}, u32[]{:S(2)}) collective-permute-start(bf16[8,24,3072]{2,1,0:T(8,128)(2,1)} %bitcast.25), channel_id=1, source_target_pairs={{248,0},{0,8},{8,16},{16,24},{24,32},{32,40},{40,48},{48,56},{56,6... | collective-permute-start | bytes 3538952 | tf_op jit(solution)/shard_map/ppermute | solution.py:14
  87.4 8.8 %reduce.2 = bf16[192,3072]{1,0:T(8,128)(2,1)S(1)} reduce(bf16[192,1,3072]{2,1,0:T(2,128)(2,1)} %bitcast.135, bf16[]{:T(256)} %broadcast.39), dimensions={1}, to_apply=%bitcast.76.reduce_sub_computation | reduce | bytes 2359298
  105.9 4.5 copy.133
  110.4 9.8 %reduce.1 = bf16[192,3072]{1,0:T(8,128)(2,1)} reduce(bf16[192,1,3072]{2,1,0:T(2,128)(2,1)} %bitcast.133, bf16[]{:T(256)} %broadcast.39), dimensions={1}, to_apply=%bitcast.75.reduce_sub_computation | reduce | bytes 2359298
  122.9 4.3 all-to-all-start.2
  127.1 19.8 %collective-permute-start.2 = (bf16[8,24,3072]{2,1,0:T(8,128)(2,1)}, bf16[8,24,3072]{2,1,0:T(8,128)(2,1)}, u32[]{:S(2)}, u32[]{:S(2)}) collective-permute-start(bf16[8,24,3072]{2,1,0:T(8,128)(2,1)} %collective-permute-done.1), channel_id=1, source_target_pairs={{248,0},{0,8},{8,16},{16,24},{24,32},{32,40},{40,48},{48,56},{56,6... | collective-permute-start | bytes 3538952 | tf_op jit(solution)/shard_map/ppermute | solution.py:14
  151.9 5.9 %reshape.161 = bf16[192,1,3072]{2,1,0:T(2,128)(2,1)} reshape(bf16[8,2,36864]{2,1,0:T(2,128)(2,1)} %all-to-all-done.2) | data formatting | bytes 2359296
  157.8 36.0 %collective-permute-start.5 = (bf16[8,24,3072]{2,1,0:T(8,128)(2,1)}, bf16[8,24,3072]{2,1,0:T(8,128)(2,1)S(1)}, u32[]{:S(2)}, u32[]{:S(2)}) collective-permute-start(bf16[8,24,3072]{2,1,0:T(8,128)(2,1)} %collective-permute-done.4), channel_id=1, source_target_pairs={{248,0},{0,8},{8,16},{16,24},{24,32},{32,40},{40,48},{48,56},{56,6... | collective-permute-start | bytes 3538952 | tf_op jit(solution)/shard_map/ppermute | solution.py:14
  197.4 5.0 pad_maximum_fusion
  202.4 4.9 collective-permute-done.5
  207.3 4.3 pad_maximum_fusion.1
  212.7 4.8 broadcast.30.clone2
  217.5 4.8 broadcast.30.clone
  222.4 98.3 %while.17 = (s32[]{:T(128)}, bf16[192,3072]{1,0:T(8,128)(2,1)}, f32[768,3072]{1,0:T(8,128)}, f32[768,3072]{1,0:T(8,128)}, bf16[768,3072]{1,0:T(8,128)(2,1)}, /*i...) while((s32[]{:T(128)}, bf16[192,3072]{1,0:T(8,128)(2,1)}, ...), condition=%wide.region_4.0_spmd, body=%wide.region_0.0_spmd.sunk | while | flops 1832580096 | bytes 128256384 | solution.py:109
  327.5 51.8 %collective-permute-done.9 = f32[192,3072]{1,0:T(8,128)S(1)} collective-permute-done((f32[192,3072]{1,0:T(8,128)S(1)}, f32[192,3072]{1,0:T(8,128)S(1)}, u32[]{:S(2)}, u32[]{:S(2)}) %collective-permute-start.9) | collective-permute-done | bytes 2359328 | tf_op jit(solution)/shard_map/ppermute | solution.py:14
  379.3 98.4 %collective-permute-done.11 = f32[192,3072]{1,0:T(8,128)} collective-permute-done((f32[192,3072]{1,0:T(8,128)S(1)}, f32[192,3072]{1,0:T(8,128)}, u32[]{:S(2)}, u32[]{:S(2)}) %collective-permute-start.11) | collective-permute-done | bytes 2359328 | tf_op jit(solution)/shard_map/ppermute | solution.py:14
  477.7 4.2 add_convert_fusion
  481.9 98.6 %collective-permute-done.8 = f32[192,3072]{1,0:T(8,128)S(1)} collective-permute-done((f32[192,3072]{1,0:T(8,128)S(1)}, f32[192,3072]{1,0:T(8,128)S(1)}, u32[]{:S(2)}, u32[]{:S(2)}) %collective-permute-start.8) | collective-permute-done | bytes 2359328 | tf_op jit(solution)/shard_map/ppermute | solution.py:14
  (143 shorter events, 153.7 us)
Async XLA Ops:
  13.5 24.5 %all-to-all-start = ((bf16[8,2,36864]{2,1,0:T(2,128)(2,1)}), bf16[8,2,36864]{2,1,0:T(2,128)(2,1)S(1)}, u32[]{:S(2)}, u32[]{:S(2)}) async-start(bf16[8,2,36864]{2,1,0:T(2,128)(2,1)} %reshape.156), calls=%async_computation | async-start | bytes 2359296 | tf_op jit(solution)/shard_map/all_to_all | solution.py:29
  38.1 20.7 %all-to-all-start.3 = ((bf16[8,2,36864]{2,1,0:T(2,128)(2,1)}), bf16[8,2,36864]{2,1,0:T(2,128)(2,1)}, u32[]{:S(2)}, u32[]{:S(2)}) async-start(bf16[8,2,36864]{2,1,0:T(2,128)(2,1)} %reshape.162), calls=%async_computation.3 | async-start | bytes 2359296 | tf_op jit(solution)/shard_map/all_to_all | solution.py:30
  44.9 56.5 %collective-permute-start = (bf16[8,24,3072]{2,1,0:T(8,128)(2,1)}, bf16[8,24,3072]{2,1,0:T(8,128)(2,1)}, u32[]{:S(2)}, u32[]{:S(2)}) collective-permute-start(bf16[8,24,3072]{2,1,0:T(8,128)(2,1)} %bitcast.21), channel_id=1, source_target_pairs={{248,0},{0,8},{8,16},{16,24},{24,32},{32,40},{40,48},{48,56},{56,6... | collective-permute-start | bytes 3538952 | tf_op jit(solution)/shard_map/ppermute | solution.py:14
  64.7 19.5 %copy-start.11 = (bf16[1,192,3072]{2,1,0:T(8,128)(2,1)S(1)}, bf16[1,192,3072]{2,1,0:T(8,128)(2,1)}, u32[]{:S(2)}) copy-start(bf16[1,192,3072]{2,1,0:T(8,128)(2,1)} %param.6) | copy-start | bytes 3538948
  67.8 35.4 %collective-permute-start.3 = (bf16[8,24,3072]{2,1,0:T(8,128)(2,1)}, bf16[8,24,3072]{2,1,0:T(8,128)(2,1)}, u32[]{:S(2)}, u32[]{:S(2)}) collective-permute-start(bf16[8,24,3072]{2,1,0:T(8,128)(2,1)} %bitcast.25), channel_id=1, source_target_pairs={{248,0},{0,8},{8,16},{16,24},{24,32},{32,40},{40,48},{48,56},{56,6... | collective-permute-start | bytes 3538952 | tf_op jit(solution)/shard_map/ppermute | solution.py:14
  97.8 25.0 %all-to-all-start.1 = ((bf16[8,2,36864]{2,1,0:T(2,128)(2,1)}), bf16[8,2,36864]{2,1,0:T(2,128)(2,1)S(1)}, u32[]{:S(2)}, u32[]{:S(2)}) async-start(bf16[8,2,36864]{2,1,0:T(2,128)(2,1)} %reshape.158), calls=%async_computation.1 | async-start | bytes 2359296 | tf_op jit(solution)/shard_map/all_to_all | solution.py:28
  101.4 25.7 %collective-permute-start.1 = (bf16[8,24,3072]{2,1,0:T(8,128)(2,1)}, bf16[8,24,3072]{2,1,0:T(8,128)(2,1)}, u32[]{:S(2)}, u32[]{:S(2)}) collective-permute-start(bf16[8,24,3072]{2,1,0:T(8,128)(2,1)} %collective-permute-done), channel_id=1, source_target_pairs={{248,0},{0,8},{8,16},{16,24},{24,32},{32,40},{40,48},{48,56},{56,6... | collective-permute-start | bytes 3538952 | tf_op jit(solution)/shard_map/ppermute | solution.py:14
  103.3 54.5 %collective-permute-start.4 = (bf16[8,24,3072]{2,1,0:T(8,128)(2,1)}, bf16[8,24,3072]{2,1,0:T(8,128)(2,1)}, u32[]{:S(2)}, u32[]{:S(2)}) collective-permute-start(bf16[8,24,3072]{2,1,0:T(8,128)(2,1)} %collective-permute-done.3), channel_id=1, source_target_pairs={{248,0},{0,8},{8,16},{16,24},{24,32},{32,40},{40,48},{48,56},{56,6... | collective-permute-start | bytes 3538952 | tf_op jit(solution)/shard_map/ppermute | solution.py:14
  122.9 29.1 %all-to-all-start.2 = ((bf16[8,2,36864]{2,1,0:T(2,128)(2,1)}), bf16[8,2,36864]{2,1,0:T(2,128)(2,1)}, u32[]{:S(2)}, u32[]{:S(2)}) async-start(bf16[8,2,36864]{2,1,0:T(2,128)(2,1)} %reshape.160), calls=%async_computation.2 | async-start | bytes 2359296 | tf_op jit(solution)/shard_map/all_to_all | solution.py:31
  127.1 70.2 %collective-permute-start.2 = (bf16[8,24,3072]{2,1,0:T(8,128)(2,1)}, bf16[8,24,3072]{2,1,0:T(8,128)(2,1)}, u32[]{:S(2)}, u32[]{:S(2)}) collective-permute-start(bf16[8,24,3072]{2,1,0:T(8,128)(2,1)} %collective-permute-done.1), channel_id=1, source_target_pairs={{248,0},{0,8},{8,16},{16,24},{24,32},{32,40},{40,48},{48,56},{56,6... | collective-permute-start | bytes 3538952 | tf_op jit(solution)/shard_map/ppermute | solution.py:14
  157.8 49.4 %collective-permute-start.5 = (bf16[8,24,3072]{2,1,0:T(8,128)(2,1)}, bf16[8,24,3072]{2,1,0:T(8,128)(2,1)S(1)}, u32[]{:S(2)}, u32[]{:S(2)}) collective-permute-start(bf16[8,24,3072]{2,1,0:T(8,128)(2,1)} %collective-permute-done.4), channel_id=1, source_target_pairs={{248,0},{0,8},{8,16},{16,24},{24,32},{32,40},{40,48},{48,56},{56,6... | collective-permute-start | bytes 3538952 | tf_op jit(solution)/shard_map/ppermute | solution.py:14
  197.4 9.9 %copy-start.9 = (bf16[1,192,3072]{2,1,0:T(8,128)(2,1)S(1)}, bf16[1,192,3072]{2,1,0:T(8,128)(2,1)}, u32[]{:S(2)}) copy-start(bf16[1,192,3072]{2,1,0:T(8,128)(2,1)} %copy.136) | copy-start | bytes 3538948
  240.9 3.7 copy-start.4
  262.5 3.6 copy-start
  273.7 3.7 copy-start.4
  295.1 3.6 copy-start
  306.4 3.7 copy-start.4
  320.7 5.8 copy-start.5
  324.4 54.9 %collective-permute-start.9 = (f32[192,3072]{1,0:T(8,128)S(1)}, f32[192,3072]{1,0:T(8,128)S(1)}, u32[]{:S(2)}, u32[]{:S(2)}) collective-permute-start(f32[192,3072]{1,0:T(8,128)S(1)} %get-tuple-element.193), channel_id=1, source_target_pairs={{8,0},{16,8},{24,16},{32,24},{40,32},{48,40},{56,48},{64,56},{72,6... | collective-permute-start | bytes 7077896 | tf_op jit(solution)/shard_map/ppermute | solution.py:14
  324.7 54.6 %collective-permute-start.10 = (f32[192,3072]{1,0:T(8,128)S(1)}, f32[192,3072]{1,0:T(8,128)S(1)}, u32[]{:S(2)}, u32[]{:S(2)}) collective-permute-start(f32[192,3072]{1,0:T(8,128)S(1)} %get-tuple-element.194), channel_id=1, source_target_pairs={{16,0},{24,8},{32,16},{40,24},{48,32},{56,40},{64,48},{72,56},{80,... | collective-permute-start | bytes 7077896 | tf_op jit(solution)/shard_map/ppermute | solution.py:14
  324.8 152.9 %collective-permute-start.11 = (f32[192,3072]{1,0:T(8,128)S(1)}, f32[192,3072]{1,0:T(8,128)}, u32[]{:S(2)}, u32[]{:S(2)}) collective-permute-start(f32[192,3072]{1,0:T(8,128)S(1)} %get-tuple-element.195), channel_id=1, source_target_pairs={{24,0},{32,8},{40,16},{48,24},{56,32},{64,40},{72,48},{80,56},{88,... | collective-permute-start | bytes 7077896 | tf_op jit(solution)/shard_map/ppermute | solution.py:14
  327.3 154.6 %collective-permute-start.6 = (f32[192,3072]{1,0:T(8,128)S(1)}, f32[192,3072]{1,0:T(8,128)S(1)}, u32[]{:S(2)}, u32[]{:S(2)}) collective-permute-start(f32[192,3072]{1,0:T(8,128)S(1)} %get-tuple-element.196), channel_id=1, source_target_pairs={{8,0},{16,8},{24,16},{32,24},{40,32},{48,40},{56,48},{64,56},{72,6... | collective-permute-start | bytes 7077896 | tf_op jit(solution)/shard_map/ppermute | solution.py:14
  327.4 154.5 %collective-permute-start.7 = (f32[192,3072]{1,0:T(8,128)S(1)}, f32[192,3072]{1,0:T(8,128)S(1)}, u32[]{:S(2)}, u32[]{:S(2)}) collective-permute-start(f32[192,3072]{1,0:T(8,128)S(1)} %get-tuple-element.197), channel_id=1, source_target_pairs={{16,0},{24,8},{32,16},{40,24},{48,32},{56,40},{64,48},{72,56},{80,... | collective-permute-start | bytes 7077896 | tf_op jit(solution)/shard_map/ppermute | solution.py:14
  379.3 201.2 %collective-permute-start.8 = (f32[192,3072]{1,0:T(8,128)S(1)}, f32[192,3072]{1,0:T(8,128)S(1)}, u32[]{:S(2)}, u32[]{:S(2)}) collective-permute-start(f32[192,3072]{1,0:T(8,128)S(1)} %get-tuple-element.198), channel_id=1, source_target_pairs={{24,0},{32,8},{40,16},{48,24},{56,32},{64,40},{72,48},{80,56},{88,... | collective-permute-start | bytes 7077896 | tf_op jit(solution)/shard_map/ppermute | solution.py:14
  (18 other events, 43.3 us)
where the time goes:
time: 591 us; the launch traced here: 583 us
  waiting for transfers between devices  271 us (46%)
  local copies, waits for them, and re-layouts  129 us (22%)
  starting transfers between devices  96.6 us (16%)
  other arithmetic  53.6 us (9%)
  matrix products  31 us (5%)
    ppermute x12, waiting for transfers between devices, shifted(): return lax.ppermute(block, axis, route)  256 us
    ppermute x12, starting transfers between devices, shifted(): return lax.ppermute(block, axis, route)  77.7 us
    unnamed x28, local copies, waits for them, and re-layouts  50.1 us
    unnamed x4, other arithmetic  35 us
    dynamic_slice x9, local copies, waits for them, and re-layouts, cut(): lax.dynamic_slice_in_dim(source, offset, group_width, 1)  20.7 us
    dynamic_update_slice x6, local copies, waits for them, and re-layouts, one_group(): lax.dynamic_update_slice_in_dim(grad_v, part_v.reshape(4 * row_count, gro...  17.1 us
    dynamic_update_slice x6, local copies, waits for them, and re-layouts, one_group(): lax.dynamic_update_slice_in_dim(grad_k, part_k.reshape(4 * row_count, gro...  13.2 us
  transfers between devices with their start and end apart: 16, of which 8 were waited for; matrix products, arithmetic and copies ran while one was open for 14% of the time, Pallas kernels for 0%

commit v1 on v0

v1 whole, which is shorter than its diff:
```python
import math

import jax
import jax.numpy as jnp
from jax import lax
from jax.experimental import pallas as pl
from jax.experimental.pallas import tpu as pltpu
from jax.sharding import Mesh, PartitionSpec as P

DH = 128
HEADS = 24
FRAMES = 8
SPOTS = 24
GROUP = 4
PLANES = 8
ROWS = FRAMES * SPOTS
OWN = GROUP * ROWS
HALO = 3 * ROWS
MINE = HEADS // GROUP
CHUNKS = (3, 3)
SCALE = 1.0 / math.sqrt(DH)
SCALE2 = SCALE * math.log2(math.e)
BF16 = jnp.bfloat16
F32 = jnp.float32
ANY = pl.BlockSpec(memory_space=pl.ANY)


def nt(a, b):
    return lax.dot_general(a, b, (((1,), (1,)), ((), ())), preferred_element_type=F32)


def nn(a, b):
    return lax.dot_general(a, b, (((1,), (0,)), ((), ())), preferred_element_type=F32)


def tn(a, b):
    return lax.dot_general(a, b, (((0,), (0,)), ((), ())), preferred_element_type=F32)


def pack_kernel(first, heads, *refs):
    sources, (packed, sems) = refs[:4], refs[4:]
    width = heads * DH
    copies = []
    for group in range(GROUP):
        for index, source in enumerate(sources):
            start = (group * MINE + first) * DH
            copies.append(
                pltpu.make_async_copy(
                    source.at[:, :, pl.ds(start, width)],
                    packed.at[group, :, :, pl.ds(index * width, width)],
                    sems.at[group * 4 + index],
                )
            )
    for copy in copies:
        copy.start()
    for copy in copies:
        copy.wait()


def pack(sources, first, heads):
    def body(*refs):
        pack_kernel(first, heads, *refs)

    return pl.pallas_call(
        body,
        out_shape=jax.ShapeDtypeStruct((GROUP, FRAMES, SPOTS, 4 * heads * DH), BF16),
        in_specs=[ANY] * 4,
        out_specs=ANY,
        scratch_shapes=[pltpu.SemaphoreType.DMA((16,))],
        name="pack",
    )(*sources)


def own_kernel(q, k, v, g, hk, hv, dq, dk, dv, stats, kx, vx):
    kx[:HALO] = hk[...]
    kx[HALO:] = k[...]
    vx[:HALO] = hv[...]
    vx[HALO:] = v[...]
    for slab in range(GROUP):
        here = slice(slab * ROWS, (slab + 1) * ROWS)
        seen = slice(slab * ROWS, (slab + 4) * ROWS)
        qs, gs = q[here], g[here]
        ks, vs = kx[seen], vx[seen]
        scores = nt(ks, qs)
        peak = jnp.max(scores, axis=0, keepdims=True) * SCALE2
        weights = jnp.exp2(scores * SCALE2 - peak)
        total = jnp.sum(weights, axis=0, keepdims=True)
        probs = weights * (1.0 / total)
        dprobs = nt(vs, gs)
        delta = jnp.sum(probs * dprobs, axis=0, keepdims=True)
        dscores = (probs * (dprobs - delta)).astype(BF16)
        low = probs.astype(BF16)
        stats[0, 2 * slab : 2 * slab + 1] = peak + jnp.log2(total)
        stats[0, 2 * slab + 1 : 2 * slab + 2] = delta
        dq[here] = (tn(dscores, ks) * SCALE).astype(BF16)
        part_k = nn(dscores[(3 - slab) * ROWS :], qs)
        part_v = nn(low[(3 - slab) * ROWS :], gs)
        if slab:
            dk[: slab * ROWS] += part_k[: slab * ROWS]
            dv[: slab * ROWS] += part_v[: slab * ROWS]
        dk[here] = part_k[slab * ROWS :]
        dv[here] = part_v[slab * ROWS :]


def own_pass(rows, halo, heads):
    def col(index):
        return pl.BlockSpec((OWN, DH), lambda h: (0, index * heads + h))

    def halo_col(index):
        return pl.BlockSpec((HALO, DH), lambda h: (0, index * heads + h))

    out = pl.BlockSpec((OWN, DH), lambda h: (0, h))
    return pl.pallas_call(
        own_kernel,
        grid=(heads,),
        in_specs=[col(2), col(0), col(1), col(3), halo_col(0), halo_col(1)],
        out_specs=[out, out, out, pl.BlockSpec((1, 8, ROWS), lambda h: (h, 0, 0))],
        out_shape=[
            jax.ShapeDtypeStruct((OWN, heads * DH), BF16),
            jax.ShapeDtypeStruct((OWN, heads * DH), F32),
            jax.ShapeDtypeStruct((OWN, heads * DH), F32),
            jax.ShapeDtypeStruct((heads, 8, ROWS), F32),
        ],
        scratch_shapes=[pltpu.VMEM((OWN + HALO, DH), BF16)] * 2,
        compiler_params=pltpu.CompilerParams(vmem_limit_bytes=40 << 20),
        cost_estimate=pl.CostEstimate(
            flops=heads * 16 * 2 * 5 * ROWS * ROWS * DH * 4,
            bytes_accessed=heads * OWN * DH * 24,
            transcendentals=heads * 16 * ROWS * ROWS,
        ),
        name="own_pass",
    )(rows, rows, rows, rows, halo, halo)


def later_kernel(k, v, hq, hg, stats, dk, dv, out, sk, sv):
    sk[...] = dk[...]
    sv[...] = dv[...]
    for slab in range(3):
        there = slice(slab * ROWS, (slab + 1) * ROWS)
        rest = slice((slab + 1) * ROWS, OWN)
        qs, gs = hq[there], hg[there]
        lse = stats[0, 2 * slab : 2 * slab + 1]
        delta = stats[0, 2 * slab + 1 : 2 * slab + 2]
        probs = jnp.exp2(nt(k[rest], qs) * SCALE2 - lse)
        dscores = (probs * (nt(v[rest], gs) - delta)).astype(BF16)
        sk[rest] += nn(dscores, qs)
        sv[rest] += nn(probs.astype(BF16), gs)
    for slab in range(GROUP):
        here = slice(slab * ROWS, (slab + 1) * ROWS)
        out[slab, 0] = (sk[here] * SCALE).astype(BF16)
        out[slab, 1] = sv[here].astype(BF16)


def later_pass(rows, halo, stats, dk, dv, heads):
    def col(index):
        return pl.BlockSpec((OWN, DH), lambda h: (0, index * heads + h))

    def halo_col(index):
        return pl.BlockSpec((HALO, DH), lambda h: (0, index * heads + h))

    return pl.pallas_call(
        later_kernel,
        grid=(heads,),
        in_specs=[
            col(0),
            col(1),
            halo_col(0),
            halo_col(1),
            pl.BlockSpec((1, 8, ROWS), lambda h: (h, 0, 0)),
            col(0),
            col(0),
        ],
        out_specs=pl.BlockSpec((GROUP, 2, ROWS, DH), lambda h: (0, 0, 0, h)),
        out_shape=jax.ShapeDtypeStruct((GROUP, 2, ROWS, heads * DH), BF16),
        scratch_shapes=[pltpu.VMEM((OWN, DH), F32)] * 2,
        compiler_params=pltpu.CompilerParams(vmem_limit_bytes=40 << 20),
        cost_estimate=pl.CostEstimate(
            flops=heads * 6 * 2 * 4 * ROWS * ROWS * DH * 4,
            bytes_accessed=heads * OWN * DH * 20,
            transcendentals=heads * 6 * ROWS * ROWS,
        ),
        name="later_pass",
    )(rows, rows, halo, halo, stats, dk, dv)


def unpack_kernel(*refs):
    count = len(CHUNKS)
    pieces_q, pieces_kv = refs[:count], refs[count : 2 * count]
    out_q, out_k, out_v, sems = refs[2 * count :]
    copies = []
    first = 0
    for chunk, heads in enumerate(CHUNKS):
        for group in range(GROUP):
            place = pl.ds((group * MINE + first) * DH, heads * DH)
            for source, target in (
                (pieces_q[chunk].at[group], out_q),
                (pieces_kv[chunk].at[group, 0], out_k),
                (pieces_kv[chunk].at[group, 1], out_v),
            ):
                copies.append(
                    pltpu.make_async_copy(source, target.at[:, place], sems.at[len(copies)])
                )
        first += heads
    for copy in copies:
        copy.start()
    for copy in copies:
        copy.wait()


def unpack(pieces_q, pieces_kv):
    shape = jax.ShapeDtypeStruct((ROWS, HEADS * DH), BF16)
    return pl.pallas_call(
        unpack_kernel,
        out_shape=[shape] * 3,
        in_specs=[ANY] * (2 * len(CHUNKS)),
        out_specs=[ANY] * 3,
        scratch_shapes=[pltpu.SemaphoreType.DMA((len(CHUNKS) * GROUP * 3,))],
        name="unpack",
    )(*pieces_q, *pieces_kv)


def to_plane(block, step):
    return lax.ppermute(block, "z", [(i, (i + step) % PLANES) for i in range(PLANES)])


def shards(queries, keys, values, grad_out):
    sources = [a.reshape(FRAMES, SPOTS, HEADS * DH) for a in (keys, values, queries, grad_out)]
    pieces_q, pieces_kv = [], []
    first = 0
    for heads in CHUNKS:
        width = heads * DH
        packed = pack(sources, first, heads).reshape(GROUP * FRAMES, SPOTS, 4 * width)
        got = lax.all_to_all(packed, ("g", "tile"), 0, 0, tiled=True)
        rows = got.reshape(OWN, 4 * width)
        earlier = to_plane(rows[ROWS:, : 2 * width], 1)
        later = to_plane(rows[:HALO, 2 * width :], -1)
        dq, dk, dv, stats = own_pass(rows, earlier, heads)
        later_stats = to_plane(stats, -1)
        dkv = later_pass(rows, later, later_stats, dk, dv, heads)
        pieces_q.append(lax.all_to_all(dq.reshape(GROUP, ROWS, width), "g", 0, 0, tiled=True))
        pieces_kv.append(lax.all_to_all(dkv, "g", 0, 0, tiled=True))
        first += heads
    outs = unpack(pieces_q, pieces_kv)
    return tuple(out.reshape(FRAMES, SPOTS, HEADS * DH) for out in outs)


def solution(mesh):
    parted = Mesh(mesh.devices.reshape(PLANES, GROUP, FRAMES), ("z", "g", "tile"))
    given = P(("z", "g", "tile"), None, None)
    wanted = P(("z", "g"), "tile", None)
    return jax.shard_map(
        shards, mesh=parted, in_specs=(given,) * 4, out_specs=(wanted,) * 3, check_vma=False
    )
```

time: 591 us -> 403 us (0.68)
  the two profiles are of different devices: /device:TPU:33 before, /device:TPU:1 now
where the time goes in v1:
time: 403 us; the launch traced here: 402 us
  Pallas kernels  289 us (72%)
  starting transfers between devices  45.1 us (11%)
  waiting for transfers between devices  32.4 us (8%)
  blocking collectives  18.8 us (5%)
  local copies, waits for them, and re-layouts  16.3 us (4%)
    pallas_call x2, Pallas kernels, pack(): pl.pallas_call(body, out_shape=jax.ShapeDtypeStruct((GROUP, FRAMES, SPOTS...  145 us
    pallas_call x1, Pallas kernels, unpack(): pl.pallas_call(unpack_kernel, out_shape=[shape] * 3, in_specs=[ANY] * (2...  109 us
    all_to_all x2, waiting for transfers between devices, shards(): got = lax.all_to_all(packed, ('g', 'tile'), 0, 0, tiled=True)  26.5 us
    pallas_call x2, Pallas kernels, own_pass(): pl.pallas_call(own_kernel, grid=(heads,), in_specs=[col(2), col(0), col(1...  26.4 us
    all_to_all x1, blocking collectives, shards(): pieces_kv.append(lax.all_to_all(dkv, 'g', 0, 0, tiled=True))  18.8 us
    all_to_all x2, starting transfers between devices, shards(): got = lax.all_to_all(packed, ('g', 'tile'), 0, 0, tiled=True)  16 us
    ppermute x6, starting transfers between devices, to_plane(): lax.ppermute(block, 'z', [(i, (i + step) % PLANES) for i in range(PLANES)])  12.9 us
    unnamed x22, local copies, waits for them, and re-layouts  12.2 us
  transfers between devices with their start and end apart: 11, of which 5 were waited for; matrix products, arithmetic and copies ran while one was open for 1% of the time, Pallas kernels for 27%

profile of v1, /device:TPU:1, one launch (start us, length us, event | category | flops | bytes accessed | tf_op | source)
XLA Modules:
  0.0 402.4 jit_solution(2401708902282794069)
XLA Ops:
  0.6 72.7 %pack.3 = bf16[4,8,24,1536]{3,2,1,0:T(8,128)(2,1)} custom-call(bf16[8,24,3072]{2,1,0:T(8,128)(2,1)} %bitcast.29, bf16[8,24,3072]{2,1,0:T(8,128)(2,1)} %bitcast.31, bf16[8,24,3072]{2,1,0:T(8,128)(2,1)} %bitcast.33, bf16[8,24,3072]{2,1,0:T(8,128)(2,1)} %bitcast.35), custom_call_target="tpu_custom_call" | custom-call | tf_op jit(solution)/shard_map/pack/pallas_call | solution.py:64
  73.4 8.6 %all-to-all-start.2 = ((bf16[32,24,1536]{2,1,0:T(8,128)(2,1)}), bf16[32,24,1536]{2,1,0:T(8,128)(2,1)S(1)}, u32[]{:S(2)}, u32[]{:S(2)}) async-start(bf16[32,24,1536]{2,1,0:T(8,128)(2,1)} %bitcast.28), calls=%async_computation.2 | async-start | bytes 4718592 | tf_op jit(solution)/shard_map/all_to_all | solution.py:233
  82.0 72.7 %pack.2 = bf16[4,8,24,1536]{3,2,1,0:T(8,128)(2,1)} custom-call(bf16[8,24,3072]{2,1,0:T(8,128)(2,1)} %bitcast.30, bf16[8,24,3072]{2,1,0:T(8,128)(2,1)} %bitcast.32, bf16[8,24,3072]{2,1,0:T(8,128)(2,1)} %bitcast.34, bf16[8,24,3072]{2,1,0:T(8,128)(2,1)} %bitcast.36), custom_call_target="tpu_custom_call" | custom-call | tf_op jit(solution)/shard_map/pack/pallas_call | solution.py:64
  154.7 1.4 copy-done
  156.1 7.4 %all-to-all-start = ((bf16[32,24,1536]{2,1,0:T(8,128)(2,1)}), bf16[32,24,1536]{2,1,0:T(8,128)(2,1)S(1)}, u32[]{:S(2)}, u32[]{:S(2)}) async-start(bf16[32,24,1536]{2,1,0:T(8,128)(2,1)} %bitcast.27), calls=%async_computation | async-start | bytes 4718592 | tf_op jit(solution)/shard_map/all_to_all | solution.py:233
  163.5 2.8 fusion
  166.2 1.6 collective-permute-start.1
  167.9 26.5 %all-to-all-done = bf16[32,24,1536]{2,1,0:T(8,128)(2,1)S(1)} async-done(((bf16[32,24,1536]{2,1,0:T(8,128)(2,1)}), bf16[32,24,1536]{2,1,0:T(8,128)(2,1)S(1)}, u32[]{:S(2)}, u32[]{:S(2)}) %all-to-all-start) | async-done | bytes 2359328 | tf_op jit(solution)/shard_map/all_to_all | solution.py:233
  195.7 1.6 collective-permute-start
  197.3 3.9 collective-permute-start.4
  201.3 13.2 %own_pass.3 = (bf16[768,384]{1,0:T(8,128)(2,1)}, f32[768,384]{1,0:T(8,128)S(1)}, f32[768,384]{1,0:T(8,128)S(1)}, f32[3,8,192]{2,1,0:T(8,128)S(1)}) custom-call(bf16[768,1536]{1,0:T(8,128)(2,1)S(1)} %bitcast.21, bf16[768,1536]{1,0:T(8,128)(2,1)S(1)} %bitcast.22, bf16[768,1536]{1,0:T(8,128)(2,1)S(1)} %bitcast.23, bf16[768,1536]{1,0:T(8,128)(2,1)S(1)} %bitcast.24, ...), custom_call_target="tpu_custom_call" | custom-call | flops 9059696640 | bytes 7077888 | tf_op jit(solution)/shard_map/own_pass/pallas_call | solution.py:113
  216.5 7.1 %all-to-all-start.3 = ((bf16[4,192,384]{2,1,0:T(8,128)(2,1)}), bf16[4,192,384]{2,1,0:T(8,128)(2,1)}, u32[]{:S(2)}, u32[]{:S(2)}) async-start(bf16[4,192,384]{2,1,0:T(8,128)(2,1)} %bitcast.9), calls=%async_computation.3 | async-start | bytes 1179648 | tf_op jit(solution)/shard_map/all_to_all | solution.py:240
  223.6 13.2 %own_pass.2 = (bf16[768,384]{1,0:T(8,128)(2,1)}, f32[768,384]{1,0:T(8,128)S(1)}, f32[768,384]{1,0:T(8,128)S(1)}, f32[3,8,192]{2,1,0:T(8,128)S(1)}) custom-call(bf16[768,1536]{1,0:T(8,128)(2,1)S(1)} %bitcast.14, bf16[768,1536]{1,0:T(8,128)(2,1)S(1)} %bitcast.15, bf16[768,1536]{1,0:T(8,128)(2,1)S(1)} %bitcast.16, bf16[768,1536]{1,0:T(8,128)(2,1)S(1)} %bitcast.17, ...), custom_call_target="tpu_custom_call" | custom-call | flops 9059696640 | bytes 7077888 | tf_op jit(solution)/shard_map/own_pass/pallas_call | solution.py:113
  238.8 4.2 %all-to-all-start.1 = ((bf16[4,192,384]{2,1,0:T(8,128)(2,1)}), bf16[4,192,384]{2,1,0:T(8,128)(2,1)}, u32[]{:S(2)}, u32[]{:S(2)}) async-start(bf16[4,192,384]{2,1,0:T(8,128)(2,1)} %bitcast.6), calls=%async_computation.1 | async-start | bytes 1179648 | tf_op jit(solution)/shard_map/all_to_all | solution.py:240
  243.0 1.9 collective-permute-start.5
  246.3 1.7 copy-done.2
  250.5 4.2 %later_pass.3 = bf16[4,2,192,384]{3,2,1,0:T(8,128)(2,1)} custom-call(bf16[768,1536]{1,0:T(8,128)(2,1)S(1)} %bitcast.25, bf16[768,1536]{1,0:T(8,128)(2,1)S(1)} %bitcast.26, bf16[576,768]{1,0:T(8,128)(2,1)S(1)} %collective-permute-done.4.hq.hg, bf16[576,768]{1,0:T(8,128)(2,1)S(1)} %collective-permute-done.4.hq.hg, ...), custom_call_target="tpu_custom_call" | custom-call | flops 2717908992 | bytes 5898240 | tf_op jit(solution)/shard_map/later_pass/pallas_call | solution.py:161
  254.7 5.1 %all-to-all-start.5 = ((bf16[4,2,192,384]{3,2,1,0:T(8,128)(2,1)}), bf16[4,2,192,384]{3,2,1,0:T(8,128)(2,1)}, u32[]{:S(2)}, u32[]{:S(2)}) async-start(bf16[4,2,192,384]{3,2,1,0:T(8,128)(2,1)} %later_pass.3), calls=%async_computation.5 | async-start | bytes 2359296 | tf_op jit(solution)/shard_map/all_to_all | solution.py:241
  259.8 3.0 collective-permute-start.3
  262.8 3.3 collective-permute-done.2.hq.hg
  269.1 4.3 %later_pass.2 = bf16[4,2,192,384]{3,2,1,0:T(8,128)(2,1)S(1)} custom-call(bf16[768,1536]{1,0:T(8,128)(2,1)S(1)} %bitcast.18, bf16[768,1536]{1,0:T(8,128)(2,1)S(1)} %bitcast.19, bf16[576,768]{1,0:T(8,128)(2,1)} %collective-permute-done.2.hq.hg, bf16[576,768]{1,0:T(8,128)(2,1)} %collective-permute-done.2.hq.hg, f32[3,8,192]{2,1,0:T(8,128)S(1)} %collective-permute-done.3.stats, ...), custom_call_target="tpu_custom_call" | custom-call | flops 2717908992 | bytes 5898240 | tf_op jit(solution)/shard_map/later_pass/pallas_call | solution.py:161
  273.5 1.4 all-to-all-done.5.refs_3_
  274.9 18.8 %all_to_all.30.refs_2_ = bf16[4,2,192,384]{3,2,1,0:T(8,128)(2,1)} all-to-all(bf16[4,2,192,384]{3,2,1,0:T(8,128)(2,1)S(1)} %later_pass.2), channel_id=1, replica_groups=mesh['z'=8,'g'=4,'tile'=8] {'g'}, dimensions={0} | all-to-all | bytes 2359296 | tf_op jit(solution)/shard_map/all_to_all | solution.py:241
  293.7 108.5 %unpack.1 = (bf16[192,3072]{1,0:T(8,128)(2,1)}, bf16[192,3072]{1,0:T(8,128)(2,1)}, bf16[192,3072]{1,0:T(8,128)(2,1)}) custom-call(bf16[4,192,384]{2,1,0:T(8,128)(2,1)} %all-to-all-done.1.refs_0_, bf16[4,192,384]{2,1,0:T(8,128)(2,1)} %all-to-all-done.3.refs_1_, bf16[4,2,192,384]{3,2,1,0:T(8,128)(2,1)} %all_to_all.30.refs_2_, ...), custom_call_target="tpu_custom_call" | custom-call | tf_op jit(solution)/shard_map/unpack/pallas_call | solution.py:212
  (30 shorter events, 12.4 us)
Async XLA Ops:
  73.4 81.3 %all-to-all-start.2 = ((bf16[32,24,1536]{2,1,0:T(8,128)(2,1)}), bf16[32,24,1536]{2,1,0:T(8,128)(2,1)S(1)}, u32[]{:S(2)}, u32[]{:S(2)}) async-start(bf16[32,24,1536]{2,1,0:T(8,128)(2,1)} %bitcast.28), calls=%async_computation.2 | async-start | bytes 4718592 | tf_op jit(solution)/shard_map/all_to_all | solution.py:233
  154.7 1.4 copy-start
  156.1 38.2 %all-to-all-start = ((bf16[32,24,1536]{2,1,0:T(8,128)(2,1)}), bf16[32,24,1536]{2,1,0:T(8,128)(2,1)S(1)}, u32[]{:S(2)}, u32[]{:S(2)}) async-start(bf16[32,24,1536]{2,1,0:T(8,128)(2,1)} %bitcast.27), calls=%async_computation | async-start | bytes 4718592 | tf_op jit(solution)/shard_map/all_to_all | solution.py:233
  166.2 35.0 %collective-permute-start.1 = (bf16[576,768]{1,0:T(8,128)(2,1)}, bf16[576,768]{1,0:T(8,128)(2,1)}, u32[]{:S(2)}, u32[]{:S(2)}) collective-permute-start(bf16[576,768]{1,0:T(8,128)(2,1)} %get-tuple-element.26), channel_id=1, source_target_pairs={{0,32},{32,64},{64,96},{96,128},{128,160},{160,192},{192,224},{224... | collective-permute-start | bytes 2654216 | tf_op jit(solution)/shard_map/ppermute | solution.py:223
  194.4 6.9 %copy-start.1 = (bf16[32,24,1536]{2,1,0:T(8,128)(2,1)S(1)}, bf16[32,24,1536]{2,1,0:T(8,128)(2,1)}, u32[]{:S(2)}) copy-start(bf16[32,24,1536]{2,1,0:T(8,128)(2,1)} %copy-done) | copy-start | bytes 7077892
  195.7 27.9 %collective-permute-start = (bf16[576,768]{1,0:T(8,128)(2,1)}, bf16[576,768]{1,0:T(8,128)(2,1)}, u32[]{:S(2)}, u32[]{:S(2)}) collective-permute-start(bf16[576,768]{1,0:T(8,128)(2,1)} %get-tuple-element.28), channel_id=1, source_target_pairs={{0,32},{32,64},{64,96},{96,128},{128,160},{160,192},{192,224},{224... | collective-permute-start | bytes 2654216 | tf_op jit(solution)/shard_map/ppermute | solution.py:223
  197.3 48.4 %collective-permute-start.4 = (bf16[576,768]{1,0:T(8,128)(2,1)}, bf16[576,768]{1,0:T(8,128)(2,1)S(1)}, u32[]{:S(2)}, u32[]{:S(2)}) collective-permute-start(bf16[576,768]{1,0:T(8,128)(2,1)} %get-tuple-element.25), channel_id=1, source_target_pairs={{0,224},{32,0},{64,32},{96,64},{128,96},{160,128},{192,160},{224,1... | collective-permute-start | bytes 2654216 | tf_op jit(solution)/shard_map/ppermute | solution.py:223
  214.5 1.0 copy-start.7
  215.5 1.0 copy-start.9
  216.5 22.3 %all-to-all-start.3 = ((bf16[4,192,384]{2,1,0:T(8,128)(2,1)}), bf16[4,192,384]{2,1,0:T(8,128)(2,1)}, u32[]{:S(2)}, u32[]{:S(2)}) async-start(bf16[4,192,384]{2,1,0:T(8,128)(2,1)} %bitcast.9), calls=%async_computation.3 | async-start | bytes 1179648 | tf_op jit(solution)/shard_map/all_to_all | solution.py:240
  236.8 1.0 copy-start.3
  237.8 1.0 copy-start.5
  238.8 15.9 %all-to-all-start.1 = ((bf16[4,192,384]{2,1,0:T(8,128)(2,1)}), bf16[4,192,384]{2,1,0:T(8,128)(2,1)}, u32[]{:S(2)}, u32[]{:S(2)}) async-start(bf16[4,192,384]{2,1,0:T(8,128)(2,1)} %bitcast.6), calls=%async_computation.1 | async-start | bytes 1179648 | tf_op jit(solution)/shard_map/all_to_all | solution.py:240
  243.0 3.3 collective-permute-start.5
  245.0 21.1 %collective-permute-start.2 = (bf16[576,768]{1,0:T(8,128)(2,1)}, bf16[576,768]{1,0:T(8,128)(2,1)}, u32[]{:S(2)}, u32[]{:S(2)}) collective-permute-start(bf16[576,768]{1,0:T(8,128)(2,1)} %get-tuple-element.27), channel_id=1, source_target_pairs={{0,224},{32,0},{64,32},{96,64},{128,96},{160,128},{192,160},{224,1... | collective-permute-start | bytes 2654216 | tf_op jit(solution)/shard_map/ppermute | solution.py:223
  246.3 1.7 copy-start.2
  248.0 1.3 copy-start.8
  249.3 1.3 copy-start.10
  254.7 20.2 %all-to-all-start.5 = ((bf16[4,2,192,384]{3,2,1,0:T(8,128)(2,1)}), bf16[4,2,192,384]{3,2,1,0:T(8,128)(2,1)}, u32[]{:S(2)}, u32[]{:S(2)}) async-start(bf16[4,2,192,384]{3,2,1,0:T(8,128)(2,1)} %later_pass.3), calls=%async_computation.5 | async-start | bytes 2359296 | tf_op jit(solution)/shard_map/all_to_all | solution.py:241
  259.8 6.8 %collective-permute-start.3 = (f32[3,8,192]{2,1,0:T(8,128)S(1)}, f32[3,8,192]{2,1,0:T(8,128)S(1)}, u32[]{:S(2)}, u32[]{:S(2)}) collective-permute-start(f32[3,8,192]{2,1,0:T(8,128)S(1)} %get-tuple-element.16), channel_id=1, source_target_pairs={{0,224},{32,0},{64,32},{96,64},{128,96},{160,128},{192,160},{224,1... | collective-permute-start | bytes 55304 | tf_op jit(solution)/shard_map/ppermute | solution.py:223
  266.6 1.3 copy-start.4
  267.9 1.3 copy-start.6

commit v2 on v1

v2 whole, which is shorter than its diff:
```python
import math

import jax
import jax.numpy as jnp
from jax import lax
from jax.experimental import pallas as pl
from jax.experimental.pallas import tpu as pltpu
from jax.sharding import Mesh, PartitionSpec as P

DH = 128
HEADS = 24
FRAMES = 8
SPOTS = 24
GROUP = 4
PLANES = 8
ROWS = FRAMES * SPOTS
OWN = GROUP * ROWS
HALO = 3 * ROWS
MINE = HEADS // GROUP
CHUNKS = (3, 3)
SCALE = 1.0 / math.sqrt(DH)
SCALE2 = SCALE * math.log2(math.e)
BF16 = jnp.bfloat16
F32 = jnp.float32
ANY = pl.BlockSpec(memory_space=pl.ANY)
PLACE = pl.BlockSpec(memory_space=pltpu.SMEM)


def nt(a, b):
    return lax.dot_general(a, b, (((1,), (1,)), ((), ())), preferred_element_type=F32)


def nn(a, b):
    return lax.dot_general(a, b, (((1,), (0,)), ((), ())), preferred_element_type=F32)


def tn(a, b):
    return lax.dot_general(a, b, (((0,), (0,)), ((), ())), preferred_element_type=F32)


def pack_kernel(parts, *refs):
    sources, (packed, held, sems) = refs[: len(parts)], refs[len(parts) :]
    loads, stores = [], []
    column = 0
    for index, (source, (_, first, heads)) in enumerate(zip(sources, parts)):
        width = heads * DH
        for group in range(GROUP):
            place = index * GROUP + group
            start = (group * MINE + first) * DH
            slot = held.at[place, :, :, pl.ds(0, width)]
            loads.append(
                pltpu.make_async_copy(
                    source.at[:, :, pl.ds(start, width)], slot, sems.at[0, place]
                )
            )
            stores.append(
                pltpu.make_async_copy(
                    slot, packed.at[group, :, :, pl.ds(column, width)], sems.at[1, place]
                )
            )
        column += width
    for load in loads:
        load.start()
    for load, store in zip(loads, stores):
        load.wait()
        store.start()
    for store in stores:
        store.wait()


def pack(tensors, parts):
    def body(*refs):
        pack_kernel(parts, *refs)

    count = len(parts) * GROUP
    most = max(heads for _, _, heads in parts)
    total = sum(heads for _, _, heads in parts)
    packed = pl.pallas_call(
        body,
        out_shape=jax.ShapeDtypeStruct((GROUP, FRAMES, SPOTS, total * DH), BF16),
        in_specs=[ANY] * len(parts),
        out_specs=ANY,
        scratch_shapes=[
            pltpu.VMEM((count, FRAMES, SPOTS, most * DH), BF16),
            pltpu.SemaphoreType.DMA((2, count)),
        ],
        compiler_params=pltpu.CompilerParams(vmem_limit_bytes=60 << 20),
        name="pack",
    )(*[tensors[name] for name, _, _ in parts])
    return packed.reshape(GROUP * FRAMES, SPOTS, total * DH)


def partner_of(place, partner):
    return lax.bitwise_xor(place, jnp.int32(partner))


def partner_rows(place, partner):
    return pl.ds(pl.multiple_of(partner_of(place[0], partner) * ROWS, ROWS), ROWS)


def slab_rows(first, count=1):
    return slice(first * ROWS, (first + count) * ROWS)


def own_kernel(place, q, k, v, g, hk, hv, *refs):
    (dk, dv, stats), dq_to, (dq, kx, vx) = refs[:3], refs[3:7], refs[7:]
    kx[:HALO] = hk[...]
    kx[HALO:] = k[...]
    vx[:HALO] = hv[...]
    vx[HALO:] = v[...]
    fronts = []
    for slab in range(GROUP):
        here, seen = slab_rows(slab), slab_rows(slab, 4)
        fronts.append((nt(kx[seen], q[here]), nt(vx[seen], g[here])))
    for slab, (scores, dprobs) in enumerate(fronts):
        here, seen, past = slab_rows(slab), slab_rows(slab, 4), slab * ROWS
        peak = jnp.max(scores, axis=0, keepdims=True) * SCALE2
        weights = jnp.exp2(scores * SCALE2 - peak)
        total = jnp.sum(weights, axis=0, keepdims=True)
        probs = weights * (1.0 / total)
        delta = jnp.sum(probs * dprobs, axis=0, keepdims=True)
        dscores = (probs * (dprobs - delta)).astype(BF16)
        low = probs.astype(BF16)
        stats[0, 2 * slab : 2 * slab + 1] = peak + jnp.log2(total)
        stats[0, 2 * slab + 1 : 2 * slab + 2] = delta
        dq[here] = (tn(kx[seen], dscores).T * SCALE).astype(BF16)
        part_k = nn(dscores[HALO - past :], q[here])
        part_v = nn(low[HALO - past :], g[here])
        if slab:
            dk[0, :past] += part_k[:past]
            dv[0, :past] += part_v[:past]
        dk[0, here] = part_k[past:]
        dv[0, here] = part_v[past:]
    for partner, target in enumerate(dq_to):
        target[...] = dq[partner_rows(place, partner)]


def own_pass(place, rows, halo, heads, room):
    def col(start, rows=OWN):
        return pl.BlockSpec((rows, DH), lambda h: (0, start + h))

    part = pl.BlockSpec((1, OWN, DH), lambda h: (h, 0, 0))
    return pl.pallas_call(
        own_kernel,
        grid=(heads,),
        in_specs=[
            PLACE,
            col(2 * heads),
            col(0),
            col(heads),
            col(3 * heads),
            col(0, HALO),
            col(heads, HALO),
        ],
        out_specs=[part, part, pl.BlockSpec((1, 8, ROWS), lambda h: (h, 0, 0))]
        + [col(0, ROWS)] * GROUP,
        out_shape=[
            jax.ShapeDtypeStruct((heads, OWN, DH), F32),
            jax.ShapeDtypeStruct((heads, OWN, DH), F32),
            jax.ShapeDtypeStruct((heads, 8, ROWS), F32),
        ]
        + [jax.ShapeDtypeStruct((ROWS, heads * DH), BF16)] * GROUP,
        scratch_shapes=[pltpu.VMEM((OWN, DH), BF16)]
        + [pltpu.VMEM((OWN + HALO, DH), BF16)] * 2,
        compiler_params=pltpu.CompilerParams(vmem_limit_bytes=room << 20),
        cost_estimate=pl.CostEstimate(
            flops=1000,
            bytes_accessed=1000,
            transcendentals=0,
        ),
        name="own_pass",
    )(place, rows, rows, rows, rows, halo, halo)


def later_kernel(place, k, v, hq, hg, stats, dk, dv, *refs):
    outs, (sk, sv) = refs[:GROUP], refs[GROUP:]
    sk[...] = dk[0]
    sv[...] = dv[0]
    fronts = []
    for slab in range(3):
        there, rest = slab_rows(slab), slice((slab + 1) * ROWS, OWN)
        fronts.append((nt(k[rest], hq[there]), nt(v[rest], hg[there])))
    for slab, (scores, dprobs) in enumerate(fronts):
        there, rest = slab_rows(slab), slice((slab + 1) * ROWS, OWN)
        lse = stats[0, 2 * slab : 2 * slab + 1]
        delta = stats[0, 2 * slab + 1 : 2 * slab + 2]
        probs = jnp.exp2(scores * SCALE2 - lse)
        dscores = (probs * (dprobs - delta)).astype(BF16)
        sk[rest] += nn(dscores, hq[there])
        sv[rest] += nn(probs.astype(BF16), hg[there])
    for partner, target in enumerate(outs):
        here = partner_rows(place, partner)
        target[0] = (sk[here] * SCALE).astype(BF16)
        target[1] = sv[here].astype(BF16)


def later_pass(place, rows, halo, stats, dk, dv, heads, room):
    def col(start, rows=OWN):
        return pl.BlockSpec((rows, DH), lambda h: (0, start + h))

    part = pl.BlockSpec((1, OWN, DH), lambda h: (h, 0, 0))
    return pl.pallas_call(
        later_kernel,
        grid=(heads,),
        in_specs=[
            PLACE,
            col(0),
            col(heads),
            col(0, HALO),
            col(heads, HALO),
            pl.BlockSpec((1, 8, ROWS), lambda h: (h, 0, 0)),
            part,
            part,
        ],
        out_specs=[pl.BlockSpec((2, ROWS, DH), lambda h: (0, 0, h))] * GROUP,
        out_shape=[jax.ShapeDtypeStruct((2, ROWS, heads * DH), BF16)] * GROUP,
        scratch_shapes=[pltpu.VMEM((OWN, DH), F32)] * 2,
        compiler_params=pltpu.CompilerParams(vmem_limit_bytes=room << 20),
        cost_estimate=pl.CostEstimate(
            flops=1000,
            bytes_accessed=1000,
            transcendentals=0,
        ),
        name="later_pass",
    )(place, rows, rows, halo, halo, stats, dk, dv)


def unpack_kernel(place, *refs):
    count = 2 * len(CHUNKS) * GROUP
    pieces, outs, (held, load_sems, store_sems) = refs[:count], refs[count : count + 3], refs[count + 3 :]
    loads = [[], [], []]
    first = 0
    for chunk, heads in enumerate(CHUNKS):
        for partner in range(GROUP):
            column = (partner_of(place[0], partner) * MINE + first) * DH
            columns = pl.ds(pl.multiple_of(column, DH), heads * DH)
            dq = pieces[2 * chunk * GROUP + partner]
            dkv = pieces[(2 * chunk + 1) * GROUP + partner]
            for index, source in enumerate((dq, dkv.at[0], dkv.at[1])):
                loads[index].append(
                    pltpu.make_async_copy(
                        source,
                        held.at[index, :, columns],
                        load_sems.at[index, chunk * GROUP + partner],
                    )
                )
        first += heads
    for load in loads[0] + loads[1] + loads[2]:
        load.start()
    stores = []
    for index in range(3):
        for load in loads[index]:
            load.wait()
        stores.append(pltpu.make_async_copy(held.at[index], outs[index], store_sems.at[index]))
        stores[-1].start()
    for store in stores:
        store.wait()


def unpack(place, pieces):
    shape = jax.ShapeDtypeStruct((ROWS, HEADS * DH), BF16)
    return pl.pallas_call(
        unpack_kernel,
        out_shape=[shape] * 3,
        in_specs=[PLACE] + [ANY] * len(pieces),
        out_specs=[ANY] * 3,
        scratch_shapes=[
            pltpu.VMEM((3, ROWS, HEADS * DH), BF16),
            pltpu.SemaphoreType.DMA((3, len(CHUNKS) * GROUP)),
            pltpu.SemaphoreType.DMA((3,)),
        ],
        compiler_params=pltpu.CompilerParams(vmem_limit_bytes=8 << 20),
        name="unpack",
    )(place, *pieces)


def edges_kernel(rows, kv, qg, held_kv, held_qg, sems):
    width = kv.shape[1]
    loads = (
        pltpu.make_async_copy(rows.at[pl.ds(ROWS, HALO), pl.ds(0, width)], held_kv, sems.at[0]),
        pltpu.make_async_copy(rows.at[pl.ds(0, HALO), pl.ds(width, width)], held_qg, sems.at[1]),
    )
    stores = (
        pltpu.make_async_copy(held_kv, kv, sems.at[2]),
        pltpu.make_async_copy(held_qg, qg, sems.at[3]),
    )
    for load in loads:
        load.start()
    for load, store in zip(loads, stores):
        load.wait()
        store.start()
    for store in stores:
        store.wait()


def edges(rows):
    width = rows.shape[1] // 2
    return pl.pallas_call(
        edges_kernel,
        out_shape=[jax.ShapeDtypeStruct((HALO, width), BF16)] * 2,
        in_specs=[ANY],
        out_specs=[ANY] * 2,
        scratch_shapes=[pltpu.VMEM((HALO, width), BF16)] * 2 + [pltpu.SemaphoreType.DMA((4,))],
        compiler_params=pltpu.CompilerParams(vmem_limit_bytes=60 << 20),
        name="edges",
    )(rows)


def to_plane(block, step):
    return lax.ppermute(block, "z", [(i, (i + step) % PLANES) for i in range(PLANES)])


def to_tiles(tensors, parts):
    got = lax.all_to_all(pack(tensors, parts), ("g", "tile"), 0, 0, tiled=True)
    return got.reshape(OWN, -1)


def to_slabs(blocks):
    sent = [
        lax.ppermute(block, "g", [(i, i ^ partner) for i in range(GROUP)])
        for partner, block in enumerate(blocks)
        if partner
    ]
    return [blocks[0], *sent]


def tied(*arrays):
    return lax.optimization_barrier(arrays)


def shards(queries, keys, values, grad_out):
    tensors = {
        name: a.reshape(FRAMES, SPOTS, HEADS * DH)
        for name, a in (("k", keys), ("v", values), ("q", queries), ("g", grad_out))
    }
    place = lax.axis_index("g").astype(jnp.int32).reshape(1)
    one, two = CHUNKS
    rows_one = to_tiles(tensors, [(name, 0, one) for name in "kvqg"])
    rows_two = to_tiles(tensors, [(name, one, two) for name in "kvqg"])

    kv_one, qg_one = edges(rows_one)
    kv_one, qg_one = to_plane(kv_one, 1), to_plane(qg_one, -1)
    dk, dv, stats, *dq = own_pass(place, rows_one, kv_one, one, 60)
    dq_one = to_slabs(dq)
    stats = to_plane(stats, -1)
    rows_two, stats = tied(rows_two, stats)
    dkv_one = to_slabs(later_pass(place, rows_one, qg_one, stats, dk, dv, one, 60))

    kv_two, qg_two = edges(rows_two)
    kv_two, qg_two = to_plane(kv_two, 1), to_plane(qg_two, -1)
    kv_two, dkv_one[0], *dq_one = tied(kv_two, dkv_one[0], *dq_one)
    dk, dv, stats, *dq = own_pass(place, rows_two, kv_two, two, 20)
    dq_two = to_slabs(dq)
    stats = to_plane(stats, -1)
    dkv = later_pass(place, rows_two, qg_two, stats, dk, dv, two, 20)
    early = tied(*dkv, *dkv_one, *dq_two)
    dkv, dkv_one, dq_two = early[:GROUP], early[GROUP : 2 * GROUP], early[2 * GROUP :]
    dkv_two = to_slabs(dkv)
    outs = unpack(place, [*dq_one, *dkv_one, *dq_two, *dkv_two])
    return tuple(out.reshape(FRAMES, SPOTS, HEADS * DH) for out in outs)


def solution(mesh):
    parted = Mesh(mesh.devices.reshape(PLANES, GROUP, FRAMES), ("z", "g", "tile"))
    given = P(("z", "g", "tile"), None, None)
    wanted = P(("z", "g"), "tile", None)
    return jax.shard_map(
        shards, mesh=parted, in_specs=(given,) * 4, out_specs=(wanted,) * 3, check_vma=False
    )
```

time: 403 us -> 158 us (0.39)
  Pallas kernels: 289 us -> 41.7 us
  waiting for transfers between devices: 32.4 us -> 71.1 us
  blocking collectives: 18.8 us -> 0 us
  local copies, waits for them, and re-layouts: 16.3 us -> 2.35 us
  starting transfers between devices: 45.1 us -> 40.9 us
    pallas_call x2, Pallas kernels: 145 us -> 5.54 us  [pack(): pl.pallas_call(body, out_shape=jax.ShapeDtypeStruct((GROUP, FRAMES, SPOTS...]
    pallas_call x5 -> x7, Pallas kernels: 143 us -> 36.2 us  [the longest x2 19.6 us: own_pass(): pl.pallas_call(own_kernel, grid=(heads,), in_specs=[PLACE, col(2 * heads)...]
    ppermute x0 -> x12, waiting for transfers between devices: none -> 20 us  [to_slabs(): lax.ppermute(block, 'g', [(i, i ^ partner) for i in range(GROUP)])]
    all_to_all x1 -> x0, blocking collectives: 18.8 us -> none  [shards(): pieces_kv.append(lax.all_to_all(dkv, 'g', 0, 0, tiled=True))]
    ppermute x6, waiting for transfers between devices: 4.48 us -> 23 us  [to_plane(): lax.ppermute(block, 'z', [(i, (i + step) % PLANES) for i in range(PLANES)])]
    all_to_all x5 -> x2, starting transfers between devices: 32.3 us -> 15 us  [to_tiles(): got = lax.all_to_all(pack(tensors, parts), ('g', 'tile'), 0, 0, tiled=True)]
    ppermute x0 -> x12, starting transfers between devices: none -> 15 us  [to_slabs(): lax.ppermute(block, 'g', [(i, i ^ partner) for i in range(GROUP)])]
    unnamed x22 -> x14, local copies, waits for them, and re-layouts: 12.2 us -> 2.35 us
  transfers between devices with their start and end apart: 11 -> 20, of which waited for: 5 -> 8; matrix products, arithmetic and copies ran while one was open for 1% -> 0% of each run, Pallas kernels for 27% -> 23%
where the time goes in v2:
time: 158 us; the launch traced here: 157 us
  waiting for transfers between devices  71.1 us (45%)
  Pallas kernels  41.7 us (26%)
  starting transfers between devices  40.9 us (26%)
  local copies, waits for them, and re-layouts  2.35 us (1%)
    all_to_all x2, waiting for transfers between devices, to_tiles(): got = lax.all_to_all(pack(tensors, parts), ('g', 'tile'), 0, 0, tiled=True)  28.1 us
    ppermute x6, waiting for transfers between devices, to_plane(): lax.ppermute(block, 'z', [(i, (i + step) % PLANES) for i in range(PLANES)])  23 us
    ppermute x12, waiting for transfers between devices, to_slabs(): lax.ppermute(block, 'g', [(i, i ^ partner) for i in range(GROUP)])  20 us
    pallas_call x2, Pallas kernels, own_pass(): pl.pallas_call(own_kernel, grid=(heads,), in_specs=[PLACE, col(2 * heads)...  19.6 us
    all_to_all x2, starting transfers between devices, to_tiles(): got = lax.all_to_all(pack(tensors, parts), ('g', 'tile'), 0, 0, tiled=True)  15 us
    ppermute x12, starting transfers between devices, to_slabs(): lax.ppermute(block, 'g', [(i, i ^ partner) for i in range(GROUP)])  15 us
    ppermute x6, starting transfers between devices, to_plane(): lax.ppermute(block, 'z', [(i, (i + step) % PLANES) for i in range(PLANES)])  10.9 us
    pallas_call x2, Pallas kernels, later_pass(): pl.pallas_call(later_kernel, grid=(heads,), in_specs=[PLACE, col(0), col(...  8.78 us
  transfers between devices with their start and end apart: 20, of which 8 were waited for; matrix products, arithmetic and copies ran while one was open for 0% of the time, Pallas kernels for 23%

profile of v2, /device:TPU:1, one launch (start us, length us, event | category | flops | bytes accessed | tf_op | source)
XLA Modules:
  0.0 157.1 jit_solution(1448970524554974320)
XLA Ops:
  0.6 2.8 %pack.3 = bf16[4,8,24,1536]{3,2,1,0:T(8,128)(2,1)} custom-call(bf16[8,24,3072]{2,1,0:T(8,128)(2,1)} %bitcast.28, bf16[8,24,3072]{2,1,0:T(8,128)(2,1)} %bitcast.30, bf16[8,24,3072]{2,1,0:T(8,128)(2,1)} %bitcast.32, bf16[8,24,3072]{2,1,0:T(8,128)(2,1)} %bitcast.34), custom_call_target="tpu_custom_call" | custom-call | tf_op jit(solution)/shard_map/pack/pallas_call | solution.py:78
  3.4 8.6 %all-to-all-start.1 = ((bf16[32,24,1536]{2,1,0:T(8,128)(2,1)}), bf16[32,24,1536]{2,1,0:T(8,128)(2,1)S(1)}, u32[]{:S(2)}, u32[]{:S(2)}) async-start(bf16[32,24,1536]{2,1,0:T(8,128)(2,1)} %bitcast.27), calls=%async_computation.1 | async-start | bytes 4718592 | tf_op jit(solution)/shard_map/all_to_all | solution.py:314
  12.0 2.8 %pack.2 = bf16[4,8,24,1536]{3,2,1,0:T(8,128)(2,1)} custom-call(bf16[8,24,3072]{2,1,0:T(8,128)(2,1)} %bitcast.29, bf16[8,24,3072]{2,1,0:T(8,128)(2,1)} %bitcast.31, bf16[8,24,3072]{2,1,0:T(8,128)(2,1)} %bitcast.33, bf16[8,24,3072]{2,1,0:T(8,128)(2,1)} %bitcast.35), custom_call_target="tpu_custom_call" | custom-call | tf_op jit(solution)/shard_map/pack/pallas_call | solution.py:78
  14.8 28.1 %all-to-all-done.1 = bf16[32,24,1536]{2,1,0:T(8,128)(2,1)S(1)} async-done(((bf16[32,24,1536]{2,1,0:T(8,128)(2,1)}), bf16[32,24,1536]{2,1,0:T(8,128)(2,1)S(1)}, u32[]{:S(2)}, u32[]{:S(2)}) %all-to-all-start.1) | async-done | bytes 2359328 | tf_op jit(solution)/shard_map/all_to_all | solution.py:314
  44.3 6.4 %all-to-all-start = ((bf16[32,24,1536]{2,1,0:T(8,128)(2,1)}), bf16[32,24,1536]{2,1,0:T(8,128)(2,1)S(1)}, u32[]{:S(2)}, u32[]{:S(2)}) async-start(bf16[32,24,1536]{2,1,0:T(8,128)(2,1)} %bitcast.26), calls=%async_computation | async-start | bytes 4718592 | tf_op jit(solution)/shard_map/all_to_all | solution.py:314
  50.7 2.4 %edges.2 = (bf16[576,768]{1,0:T(8,128)(2,1)}, bf16[576,768]{1,0:T(8,128)(2,1)}) custom-call(bf16[768,1536]{1,0:T(8,128)(2,1)} %bitcast.19), custom_call_target="tpu_custom_call" | custom-call | tf_op jit(solution)/shard_map/edges/pallas_call | solution.py:298
  53.1 1.7 %collective-permute-start = (bf16[576,768]{1,0:T(8,128)(2,1)}, bf16[576,768]{1,0:T(8,128)(2,1)S(1)}, u32[]{:S(2)}, u32[]{:S(2)}) collective-permute-start(bf16[576,768]{1,0:T(8,128)(2,1)} %get-tuple-element.52), channel_id=1, source_target_pairs={{0,32},{32,64},{64,96},{96,128},{128,160},{160,192},{192,224},{224... | collective-permute-start | bytes 2654216 | tf_op jit(solution)/shard_map/ppermute | solution.py:310
  54.9 4.0 %collective-permute-start.3 = (bf16[576,768]{1,0:T(8,128)(2,1)}, bf16[576,768]{1,0:T(8,128)(2,1)}, u32[]{:S(2)}, u32[]{:S(2)}) collective-permute-start(bf16[576,768]{1,0:T(8,128)(2,1)} %get-tuple-element.56), channel_id=1, source_target_pairs={{0,224},{32,0},{64,32},{96,64},{128,96},{160,128},{192,160},{224,1... | collective-permute-start | bytes 2654216 | tf_op jit(solution)/shard_map/ppermute | solution.py:310
  58.9 19.9 %collective-permute-done.hk.hv = bf16[576,768]{1,0:T(8,128)(2,1)S(1)} collective-permute-done((bf16[576,768]{1,0:T(8,128)(2,1)}, bf16[576,768]{1,0:T(8,128)(2,1)S(1)}, u32[]{:S(2)}, u32[]{:S(2)}) %collective-permute-start) | collective-permute-done | bytes 884768 | tf_op jit(solution)/shard_map/ppermute | solution.py:310
  79.7 10.5 %own_pass.2 = (f32[3,768,128]{2,1,0:T(8,128)}, f32[3,768,128]{2,1,0:T(8,128)}, f32[3,8,192]{2,1,0:T(8,128)}, bf16[192,384]{1,0:T(8,128)(2,1)}, bf16[192,384]{1,0...) custom-call(s32[1]{0:T(128)} %bitcast.place, bf16[768,1536]{1,0:T(8,128)(2,1)} %bitcast.20, ...), custom_call_target="tpu_custom_call" | custom-call | flops 1000 | bytes 1000 | tf_op jit(solution)/shard_map/own_pass/pallas_call | solution.py:143
  91.6 1.6 %collective-permute-done.1.stats = f32[3,8,192]{2,1,0:T(8,128)S(1)} collective-permute-done((f32[3,8,192]{2,1,0:T(8,128)}, f32[3,8,192]{2,1,0:T(8,128)S(1)}, u32[]{:S(2)}, u32[]{:S(2)}) %collective-permute-start.1) | collective-permute-done | bytes 18464 | tf_op jit(solution)/shard_map/ppermute | solution.py:310
  93.2 2.4 %edges.3 = (bf16[576,768]{1,0:T(8,128)(2,1)}, bf16[576,768]{1,0:T(8,128)(2,1)}) custom-call(bf16[768,1536]{1,0:T(8,128)(2,1)} %bitcast.12), custom_call_target="tpu_custom_call" | custom-call | tf_op jit(solution)/shard_map/edges/pallas_call | solution.py:298
  95.7 2.7 %collective-permute-start.7 = (bf16[576,768]{1,0:T(8,128)(2,1)}, bf16[576,768]{1,0:T(8,128)(2,1)S(1)}, u32[]{:S(2)}, u32[]{:S(2)}) collective-permute-start(bf16[576,768]{1,0:T(8,128)(2,1)} %get-tuple-element.69), channel_id=1, source_target_pairs={{0,224},{32,0},{64,32},{96,64},{128,96},{160,128},{192,160},{224,1... | collective-permute-start | bytes 2654216 | tf_op jit(solution)/shard_map/ppermute | solution.py:310
  98.4 2.5 %collective-permute-start.4 = (bf16[192,384]{1,0:T(8,128)(2,1)}, bf16[192,384]{1,0:T(8,128)(2,1)}, u32[]{:S(2)}, u32[]{:S(2)}) collective-permute-start(bf16[192,384]{1,0:T(8,128)(2,1)} %get-tuple-element.62), channel_id=1, source_target_pairs={{0,8},{8,0},{16,24},{24,16},{1,9},{9,1},{17,25},{25,17},{2,10},{10... | collective-permute-start | bytes 442376 | tf_op jit(solution)/shard_map/ppermute | solution.py:320
  102.4 5.6 %later_pass.2 = (bf16[2,192,384]{2,1,0:T(8,128)(2,1)}, bf16[2,192,384]{2,1,0:T(8,128)(2,1)}, bf16[2,192,384]{2,1,0:T(8,128)(2,1)}, bf16[2,192,384]{2,1,0:T(8,128)(2,1)}) custom-call(s32[1]{0:T(128)} %bitcast.place, bf16[768,1536]{1,0:T(8,128)(2,1)} %bitcast.24, bf16[768,1536]{1,0:T(8,128)(2,1)} %bitcast.25, bf16[576,768]{1,0:T(8,128)(2,1)} %collective-permute-done.3.hq.hg, ...), custom_call_target="tpu_custom_call" | custom-call | flops 1000 | bytes 1000 | tf_op jit(solution)/shard_map/later_pass/pallas_call | solution.py:202
  109.8 5.0 %collective-permute-done.6.refs_3_ = bf16[192,384]{1,0:T(8,128)(2,1)S(1)} collective-permute-done((bf16[192,384]{1,0:T(8,128)(2,1)}, bf16[192,384]{1,0:T(8,128)(2,1)S(1)}, u32[]{:S(2)}, u32[]{:S(2)}) %collective-permute-start.6) | collective-permute-done | bytes 147488 | tf_op jit(solution)/shard_map/ppermute | solution.py:320
  116.3 9.1 %own_pass.3 = (f32[3,768,128]{2,1,0:T(8,128)S(1)}, f32[3,768,128]{2,1,0:T(8,128)S(1)}, f32[3,8,192]{2,1,0:T(8,128)S(1)}, bf16[192,384]{1,0:T(8,128)(2,1)S(1)}, b...) custom-call(s32[1]{0:T(128)} %bitcast.place, ...), custom_call_target="tpu_custom_call" | custom-call | flops 1000 | bytes 1000 | tf_op jit(solution)/shard_map/own_pass/pallas_call | solution.py:143
  126.5 3.3 %collective-permute-start.12 = (bf16[192,384]{1,0:T(8,128)(2,1)S(1)}, bf16[192,384]{1,0:T(8,128)(2,1)S(1)}, u32[]{:S(2)}, u32[]{:S(2)}) collective-permute-start(bf16[192,384]{1,0:T(8,128)(2,1)S(1)} %get-tuple-element.83), channel_id=1, source_target_pairs={{0,8},{8,0},{16,24},{24,16},{1,9},{9,1},{17,25},{25,17},{2,10},{10... | collective-permute-start | bytes 442376 | tf_op jit(solution)/shard_map/ppermute | solution.py:320
  131.3 2.2 %collective-permute-start.14 = (bf16[192,384]{1,0:T(8,128)(2,1)S(1)}, bf16[192,384]{1,0:T(8,128)(2,1)S(1)}, u32[]{:S(2)}, u32[]{:S(2)}) collective-permute-start(bf16[192,384]{1,0:T(8,128)(2,1)S(1)} %get-tuple-element.85), channel_id=1, source_target_pairs={{0,24},{8,16},{16,8},{24,0},{1,25},{9,17},{17,9},{25,1},{2,26},{10... | collective-permute-start | bytes 442376 | tf_op jit(solution)/shard_map/ppermute | solution.py:320
  133.5 3.2 %later_pass.3 = (bf16[2,192,384]{2,1,0:T(8,128)(2,1)S(1)}, bf16[2,192,384]{2,1,0:T(8,128)(2,1)S(1)}, bf16[2,192,384]{2,1,0:T(8,128)(2,1)S(1)}, bf16[2,192,384]{2,1,0:T(8,128)(2,1)S(1)}) custom-call(s32[1]{0:T(128)} %bitcast.place, bf16[768,1536]{1,0:T(8,128)(2,1)S(1)} %bitcast.17, bf16[768,1536]{1,0:T(8,128)(2,1)S(1)} %bitcast.18, ...), custom_call_target="tpu_custom_call" | custom-call | flops 1000 | bytes 1000 | tf_op jit(solution)/shard_map/later_pass/pallas_call | solution.py:202
  136.7 1.9 %collective-permute-done.14.refs_11_ = bf16[192,384]{1,0:T(8,128)(2,1)S(1)} collective-permute-done((bf16[192,384]{1,0:T(8,128)(2,1)S(1)}, bf16[192,384]{1,0:T(8,128)(2,1)S(1)}, u32[]{:S(2)}, u32[]{:S(2)}) %collective-permute-start.14) | collective-permute-done | bytes 147488 | tf_op jit(solution)/shard_map/ppermute | solution.py:320
  140.8 6.4 %collective-permute-done.16.refs_14_ = bf16[2,192,384]{2,1,0:T(8,128)(2,1)S(1)} collective-permute-done((bf16[2,192,384]{2,1,0:T(8,128)(2,1)S(1)}, bf16[2,192,384]{2,1,0:T(8,128)(2,1)S(1)}, u32[]{:S(2)}, u32[]{:S(2)}) %collective-permute-start.16) | collective-permute-done | bytes 294944 | tf_op jit(solution)/shard_map/ppermute | solution.py:320
  147.2 6.7 %collective-permute-done.17.refs_15_ = bf16[2,192,384]{2,1,0:T(8,128)(2,1)S(1)} collective-permute-done((bf16[2,192,384]{2,1,0:T(8,128)(2,1)S(1)}, bf16[2,192,384]{2,1,0:T(8,128)(2,1)S(1)}, u32[]{:S(2)}, u32[]{:S(2)}) %collective-permute-start.17) | collective-permute-done | bytes 294944 | tf_op jit(solution)/shard_map/ppermute | solution.py:320
  153.9 3.0 %unpack.1 = (bf16[192,3072]{1,0:T(8,128)(2,1)}, bf16[192,3072]{1,0:T(8,128)(2,1)}, bf16[192,3072]{1,0:T(8,128)(2,1)}) custom-call(s32[1]{0:T(128)} %bitcast.place, bf16[192,384]{1,0:T(8,128)(2,1)S(1)} %copy-done.3, bf16[192,384]{1,0:T(8,128)(2,1)} %collective-permute-done.4.refs_1_, bf16[192,384]{1,0:T(8,128)(2,1)} %collective-permute-done.5.refs_2_, ...), custom_call_target="tpu_custom_call" | custom-call | tf_op jit(solution)/shard_map/unpack/pallas_call | solution.py:262
  (39 shorter events, 13.3 us)
Async XLA Ops:
  3.4 39.5 %all-to-all-start.1 = ((bf16[32,24,1536]{2,1,0:T(8,128)(2,1)}), bf16[32,24,1536]{2,1,0:T(8,128)(2,1)S(1)}, u32[]{:S(2)}, u32[]{:S(2)}) async-start(bf16[32,24,1536]{2,1,0:T(8,128)(2,1)} %bitcast.27), calls=%async_computation.1 | async-start | bytes 4718592 | tf_op jit(solution)/shard_map/all_to_all | solution.py:314
  44.3 47.3 %all-to-all-start = ((bf16[32,24,1536]{2,1,0:T(8,128)(2,1)}), bf16[32,24,1536]{2,1,0:T(8,128)(2,1)S(1)}, u32[]{:S(2)}, u32[]{:S(2)}) async-start(bf16[32,24,1536]{2,1,0:T(8,128)(2,1)} %bitcast.26), calls=%async_computation | async-start | bytes 4718592 | tf_op jit(solution)/shard_map/all_to_all | solution.py:314
  53.1 25.7 %collective-permute-start = (bf16[576,768]{1,0:T(8,128)(2,1)}, bf16[576,768]{1,0:T(8,128)(2,1)S(1)}, u32[]{:S(2)}, u32[]{:S(2)}) collective-permute-start(bf16[576,768]{1,0:T(8,128)(2,1)} %get-tuple-element.52), channel_id=1, source_target_pairs={{0,32},{32,64},{64,96},{96,128},{128,160},{160,192},{192,224},{224... | collective-permute-start | bytes 2654216 | tf_op jit(solution)/shard_map/ppermute | solution.py:310
  54.9 47.5 %collective-permute-start.3 = (bf16[576,768]{1,0:T(8,128)(2,1)}, bf16[576,768]{1,0:T(8,128)(2,1)}, u32[]{:S(2)}, u32[]{:S(2)}) collective-permute-start(bf16[576,768]{1,0:T(8,128)(2,1)} %get-tuple-element.56), channel_id=1, source_target_pairs={{0,224},{32,0},{64,32},{96,64},{128,96},{160,128},{192,160},{224,1... | collective-permute-start | bytes 2654216 | tf_op jit(solution)/shard_map/ppermute | solution.py:310
  90.2 3.0 %collective-permute-start.1 = (f32[3,8,192]{2,1,0:T(8,128)}, f32[3,8,192]{2,1,0:T(8,128)S(1)}, u32[]{:S(2)}, u32[]{:S(2)}) collective-permute-start(f32[3,8,192]{2,1,0:T(8,128)} %get-tuple-element.53), channel_id=1, source_target_pairs={{0,224},{32,0},{64,32},{96,64},{128,96},{160,128},{192,160},{224,1... | collective-permute-start | bytes 55304 | tf_op jit(solution)/shard_map/ppermute | solution.py:310
  93.2 2.4 %copy-start.6 = (f32[3,8,192]{2,1,0:T(8,128)}, f32[3,8,192]{2,1,0:T(8,128)S(1)}, u32[]{:S(2)}) copy-start(f32[3,8,192]{2,1,0:T(8,128)S(1)} %collective-permute-done.1.stats) | copy-start | bytes 55300
  95.6 20.7 %collective-permute-start.2 = (bf16[576,768]{1,0:T(8,128)(2,1)}, bf16[576,768]{1,0:T(8,128)(2,1)S(1)}, u32[]{:S(2)}, u32[]{:S(2)}) collective-permute-start(bf16[576,768]{1,0:T(8,128)(2,1)} %get-tuple-element.55), channel_id=1, source_target_pairs={{0,32},{32,64},{64,96},{96,128},{128,160},{160,192},{192,224},{224... | collective-permute-start | bytes 2654216 | tf_op jit(solution)/shard_map/ppermute | solution.py:310
  95.7 34.2 %collective-permute-start.7 = (bf16[576,768]{1,0:T(8,128)(2,1)}, bf16[576,768]{1,0:T(8,128)(2,1)S(1)}, u32[]{:S(2)}, u32[]{:S(2)}) collective-permute-start(bf16[576,768]{1,0:T(8,128)(2,1)} %get-tuple-element.69), channel_id=1, source_target_pairs={{0,224},{32,0},{64,32},{96,64},{128,96},{160,128},{192,160},{224,1... | collective-permute-start | bytes 2654216 | tf_op jit(solution)/shard_map/ppermute | solution.py:310
  98.4 9.9 %collective-permute-start.4 = (bf16[192,384]{1,0:T(8,128)(2,1)}, bf16[192,384]{1,0:T(8,128)(2,1)}, u32[]{:S(2)}, u32[]{:S(2)}) collective-permute-start(bf16[192,384]{1,0:T(8,128)(2,1)} %get-tuple-element.62), channel_id=1, source_target_pairs={{0,8},{8,0},{16,24},{24,16},{1,9},{9,1},{17,25},{25,17},{2,10},{10... | collective-permute-start | bytes 442376 | tf_op jit(solution)/shard_map/ppermute | solution.py:320
  100.9 7.5 %collective-permute-start.5 = (bf16[192,384]{1,0:T(8,128)(2,1)}, bf16[192,384]{1,0:T(8,128)(2,1)}, u32[]{:S(2)}, u32[]{:S(2)}) collective-permute-start(bf16[192,384]{1,0:T(8,128)(2,1)} %get-tuple-element.63), channel_id=1, source_target_pairs={{0,16},{8,24},{16,0},{24,8},{1,17},{9,25},{17,1},{25,9},{2,18},{10... | collective-permute-start | bytes 442376 | tf_op jit(solution)/shard_map/ppermute | solution.py:320
  102.4 14.0 %copy-start.1 = (bf16[32,24,1536]{2,1,0:T(8,128)(2,1)S(1)}, bf16[32,24,1536]{2,1,0:T(8,128)(2,1)}, u32[]{:S(2)}) copy-start(bf16[32,24,1536]{2,1,0:T(8,128)(2,1)} %copy-done) | copy-start | bytes 7077892
  107.9 18.6 %collective-permute-start.9 = (bf16[2,192,384]{2,1,0:T(8,128)(2,1)}, bf16[2,192,384]{2,1,0:T(8,128)(2,1)S(1)}, u32[]{:S(2)}, u32[]{:S(2)}) collective-permute-start(bf16[2,192,384]{2,1,0:T(8,128)(2,1)} %get-tuple-element.79), channel_id=1, source_target_pairs={{0,8},{8,0},{16,24},{24,16},{1,9},{9,1},{17,25},{25,17},{2,10},{10... | collective-permute-start | bytes 884744 | tf_op jit(solution)/shard_map/ppermute | solution.py:320
  108.3 6.6 %collective-permute-start.6 = (bf16[192,384]{1,0:T(8,128)(2,1)}, bf16[192,384]{1,0:T(8,128)(2,1)S(1)}, u32[]{:S(2)}, u32[]{:S(2)}) collective-permute-start(bf16[192,384]{1,0:T(8,128)(2,1)} %get-tuple-element.64), channel_id=1, source_target_pairs={{0,24},{8,16},{16,8},{24,0},{1,25},{9,17},{17,9},{25,1},{2,26},{10... | collective-permute-start | bytes 442376 | tf_op jit(solution)/shard_map/ppermute | solution.py:320
  108.4 28.3 %collective-permute-start.10 = (bf16[2,192,384]{2,1,0:T(8,128)(2,1)}, bf16[2,192,384]{2,1,0:T(8,128)(2,1)S(1)}, u32[]{:S(2)}, u32[]{:S(2)}) collective-permute-start(bf16[2,192,384]{2,1,0:T(8,128)(2,1)} %get-tuple-element.80), channel_id=1, source_target_pairs={{0,16},{8,24},{16,0},{24,8},{1,17},{9,25},{17,1},{25,9},{2,18},{10... | collective-permute-start | bytes 884744 | tf_op jit(solution)/shard_map/ppermute | solution.py:320
  114.8 21.9 %collective-permute-start.11 = (bf16[2,192,384]{2,1,0:T(8,128)(2,1)}, bf16[2,192,384]{2,1,0:T(8,128)(2,1)S(1)}, u32[]{:S(2)}, u32[]{:S(2)}) collective-permute-start(bf16[2,192,384]{2,1,0:T(8,128)(2,1)} %get-tuple-element.81), channel_id=1, source_target_pairs={{0,24},{8,16},{16,8},{24,0},{1,25},{9,17},{17,9},{25,1},{2,26},{10... | collective-permute-start | bytes 884744 | tf_op jit(solution)/shard_map/ppermute | solution.py:320
  125.4 5.9 %collective-permute-start.8 = (f32[3,8,192]{2,1,0:T(8,128)S(1)}, f32[3,8,192]{2,1,0:T(8,128)S(1)}, u32[]{:S(2)}, u32[]{:S(2)}) collective-permute-start(f32[3,8,192]{2,1,0:T(8,128)S(1)} %get-tuple-element.71), channel_id=1, source_target_pairs={{0,224},{32,0},{64,32},{96,64},{128,96},{160,128},{192,160},{224,1... | collective-permute-start | bytes 55304 | tf_op jit(solution)/shard_map/ppermute | solution.py:310
  126.5 10.2 %collective-permute-start.12 = (bf16[192,384]{1,0:T(8,128)(2,1)S(1)}, bf16[192,384]{1,0:T(8,128)(2,1)S(1)}, u32[]{:S(2)}, u32[]{:S(2)}) collective-permute-start(bf16[192,384]{1,0:T(8,128)(2,1)S(1)} %get-tuple-element.83), channel_id=1, source_target_pairs={{0,8},{8,0},{16,24},{24,16},{1,9},{9,1},{17,25},{25,17},{2,10},{10... | collective-permute-start | bytes 442376 | tf_op jit(solution)/shard_map/ppermute | solution.py:320
  129.9 6.9 %collective-permute-start.13 = (bf16[192,384]{1,0:T(8,128)(2,1)S(1)}, bf16[192,384]{1,0:T(8,128)(2,1)S(1)}, u32[]{:S(2)}, u32[]{:S(2)}) collective-permute-start(bf16[192,384]{1,0:T(8,128)(2,1)S(1)} %get-tuple-element.84), channel_id=1, source_target_pairs={{0,16},{8,24},{16,0},{24,8},{1,17},{9,25},{17,1},{25,9},{2,18},{10... | collective-permute-start | bytes 442376 | tf_op jit(solution)/shard_map/ppermute | solution.py:320
  131.3 7.3 %collective-permute-start.14 = (bf16[192,384]{1,0:T(8,128)(2,1)S(1)}, bf16[192,384]{1,0:T(8,128)(2,1)S(1)}, u32[]{:S(2)}, u32[]{:S(2)}) collective-permute-start(bf16[192,384]{1,0:T(8,128)(2,1)S(1)} %get-tuple-element.85), channel_id=1, source_target_pairs={{0,24},{8,16},{16,8},{24,0},{1,25},{9,17},{17,9},{25,1},{2,26},{10... | collective-permute-start | bytes 442376 | tf_op jit(solution)/shard_map/ppermute | solution.py:320
  133.5 20.4 %copy-start.2 = (bf16[2,192,384]{2,1,0:T(8,128)(2,1)S(1)}, bf16[2,192,384]{2,1,0:T(8,128)(2,1)}, u32[]{:S(2)}) copy-start(bf16[2,192,384]{2,1,0:T(8,128)(2,1)} %get-tuple-element.86.refs_4_) | copy-start | bytes 884740
  133.5 20.4 %copy-start.3 = (bf16[192,384]{1,0:T(8,128)(2,1)S(1)}, bf16[192,384]{1,0:T(8,128)(2,1)}, u32[]{:S(2)}) copy-start(bf16[192,384]{1,0:T(8,128)(2,1)} %get-tuple-element.65.refs_0_) | copy-start | bytes 442372
  138.6 2.1 %collective-permute-start.15 = (bf16[2,192,384]{2,1,0:T(8,128)(2,1)S(1)}, bf16[2,192,384]{2,1,0:T(8,128)(2,1)S(1)}, u32[]{:S(2)}, u32[]{:S(2)}) collective-permute-start(bf16[2,192,384]{2,1,0:T(8,128)(2,1)S(1)} %get-tuple-element.95), channel_id=1, source_target_pairs={{0,8},{8,0},{16,24},{24,16},{1,9},{9,1},{17,25},{25,17},{2,10},{10... | collective-permute-start | bytes 884744 | tf_op jit(solution)/shard_map/ppermute | solution.py:320
  138.8 8.3 %collective-permute-start.16 = (bf16[2,192,384]{2,1,0:T(8,128)(2,1)S(1)}, bf16[2,192,384]{2,1,0:T(8,128)(2,1)S(1)}, u32[]{:S(2)}, u32[]{:S(2)}) collective-permute-start(bf16[2,192,384]{2,1,0:T(8,128)(2,1)S(1)} %get-tuple-element.96), channel_id=1, source_target_pairs={{0,16},{8,24},{16,0},{24,8},{1,17},{9,25},{17,1},{25,9},{2,18},{10... | collective-permute-start | bytes 884744 | tf_op jit(solution)/shard_map/ppermute | solution.py:320
  140.2 13.7 %collective-permute-start.17 = (bf16[2,192,384]{2,1,0:T(8,128)(2,1)S(1)}, bf16[2,192,384]{2,1,0:T(8,128)(2,1)S(1)}, u32[]{:S(2)}, u32[]{:S(2)}) collective-permute-start(bf16[2,192,384]{2,1,0:T(8,128)(2,1)S(1)} %get-tuple-element.97), channel_id=1, source_target_pairs={{0,24},{8,16},{16,8},{24,0},{1,25},{9,17},{17,9},{25,1},{2,26},{10... | collective-permute-start | bytes 884744 | tf_op jit(solution)/shard_map/ppermute | solution.py:320
  (3 other events, 4.0 us)

commit v3 on v2

--- a/solution.py
+++ b/solution.py
@@ -135,7 +135,7 @@
         target[...] = dq[partner_rows(place, partner)]
 
 
-def own_pass(place, rows, halo, heads, room):
+def own_pass(place, rows, halo, heads, room, work=1000):
     def col(start, rows=OWN):
         return pl.BlockSpec((rows, DH), lambda h: (0, start + h))
 
@@ -164,7 +164,7 @@
         + [pltpu.VMEM((OWN + HALO, DH), BF16)] * 2,
         compiler_params=pltpu.CompilerParams(vmem_limit_bytes=room << 20),
         cost_estimate=pl.CostEstimate(
-            flops=1000,
+            flops=work,
             bytes_accessed=1000,
             transcendentals=0,
         ),
@@ -301,7 +301,7 @@
         in_specs=[ANY],
         out_specs=[ANY] * 2,
         scratch_shapes=[pltpu.VMEM((HALO, width), BF16)] * 2 + [pltpu.SemaphoreType.DMA((4,))],
-        compiler_params=pltpu.CompilerParams(vmem_limit_bytes=60 << 20),
+        compiler_params=pltpu.CompilerParams(vmem_limit_bytes=4 << 20),
         name="edges",
     )(rows)
 
@@ -310,9 +310,8 @@
     return lax.ppermute(block, "z", [(i, (i + step) % PLANES) for i in range(PLANES)])
 
 
-def to_tiles(tensors, parts):
-    got = lax.all_to_all(pack(tensors, parts), ("g", "tile"), 0, 0, tiled=True)
-    return got.reshape(OWN, -1)
+def to_tiles(packed):
+    return lax.all_to_all(packed, ("g", "tile"), 0, 0, tiled=True).reshape(OWN, -1)
 
 
 def to_slabs(blocks):
@@ -335,12 +334,14 @@
     }
     place = lax.axis_index("g").astype(jnp.int32).reshape(1)
     one, two = CHUNKS
-    rows_one = to_tiles(tensors, [(name, 0, one) for name in "kvqg"])
-    rows_two = to_tiles(tensors, [(name, one, two) for name in "kvqg"])
+    rows_one = to_tiles(pack(tensors, [(name, 0, one) for name in "kvqg"]))
+    packed_two = pack(tensors, [(name, one, two) for name in "kvqg"])
+    rows_one, packed_two = tied(rows_one, packed_two)
+    rows_two = to_tiles(packed_two)
 
     kv_one, qg_one = edges(rows_one)
     kv_one, qg_one = to_plane(kv_one, 1), to_plane(qg_one, -1)
-    dk, dv, stats, *dq = own_pass(place, rows_one, kv_one, one, 60)
+    dk, dv, stats, *dq = own_pass(place, rows_one, kv_one, one, 60, 200_000_000_000)
     dq_one = to_slabs(dq)
     stats = to_plane(stats, -1)
     rows_two, stats = tied(rows_two, stats)

time: 158 us -> 150 us (0.949)
  waiting for transfers between devices: 71.1 us -> 63.9 us
    ppermute x6, waiting for transfers between devices: 23 us -> 13.4 us  [to_plane(): lax.ppermute(block, 'z', [(i, (i + step) % PLANES) for i in range(PLANES)])]
    all_to_all x2, waiting for transfers between devices: 28.1 us -> 30.2 us  [to_tiles(): lax.all_to_all(packed, ('g', 'tile'), 0, 0, tiled=True).reshape(OWN, -1)]
    pallas_call x2, Pallas kernels: 4.82 us -> 3.14 us  [edges(): pl.pallas_call(edges_kernel, out_shape=[jax.ShapeDtypeStruct((HALO, width...]
  transfers between devices with their start and end apart: 20 -> 20, of which waited for: 8 -> 9; matrix products, arithmetic and copies ran while one was open for 0% -> 0% of each run, Pallas kernels for 23% -> 23%
where the time goes in v3:
time: 150 us; the launch traced here: 149 us
  waiting for transfers between devices  63.9 us (43%)
  starting transfers between devices  42.2 us (28%)
  Pallas kernels  41.1 us (27%)
    all_to_all x2, waiting for transfers between devices, to_tiles(): lax.all_to_all(packed, ('g', 'tile'), 0, 0, tiled=True).reshape(OWN, -1)  30.2 us
    pallas_call x2, Pallas kernels, own_pass(): pl.pallas_call(own_kernel, grid=(heads,), in_specs=[PLACE, col(2 * heads)...  20.3 us
    ppermute x12, waiting for transfers between devices, to_slabs(): lax.ppermute(block, 'g', [(i, i ^ partner) for i in range(GROUP)])  20.3 us
    all_to_all x2, starting transfers between devices, to_tiles(): lax.all_to_all(packed, ('g', 'tile'), 0, 0, tiled=True).reshape(OWN, -1)  16 us
    ppermute x12, starting transfers between devices, to_slabs(): lax.ppermute(block, 'g', [(i, i ^ partner) for i in range(GROUP)])  13.9 us
    ppermute x6, waiting for transfers between devices, to_plane(): lax.ppermute(block, 'z', [(i, (i + step) % PLANES) for i in range(PLANES)])  13.4 us
    ppermute x6, starting transfers between devices, to_plane(): lax.ppermute(block, 'z', [(i, (i + step) % PLANES) for i in range(PLANES)])  12.3 us
    pallas_call x2, Pallas kernels, later_pass(): pl.pallas_call(later_kernel, grid=(heads,), in_specs=[PLACE, col(0), col(...  9.43 us
  transfers between devices with their start and end apart: 20, of which 9 were waited for; matrix products, arithmetic and copies ran while one was open for 0% of the time, Pallas kernels for 23%

profile of v3, /device:TPU:1, one launch (start us, length us, event | category | flops | bytes accessed | tf_op | source)
XLA Modules:
  0.0 149.4 jit_solution(13427826146115325872)
XLA Ops:
  0.6 2.8 %pack.2 = bf16[4,8,24,1536]{3,2,1,0:T(8,128)(2,1)} custom-call(bf16[8,24,3072]{2,1,0:T(8,128)(2,1)} %bitcast.21, bf16[8,24,3072]{2,1,0:T(8,128)(2,1)} %bitcast.23, bf16[8,24,3072]{2,1,0:T(8,128)(2,1)} %bitcast.25, bf16[8,24,3072]{2,1,0:T(8,128)(2,1)} %bitcast.27), custom_call_target="tpu_custom_call" | custom-call | tf_op jit(solution)/shard_map/pack/pallas_call | solution.py:78
  3.4 8.6 %all-to-all-start = ((bf16[32,24,1536]{2,1,0:T(8,128)(2,1)}), bf16[32,24,1536]{2,1,0:T(8,128)(2,1)S(1)}, u32[]{:S(2)}, u32[]{:S(2)}) async-start(bf16[32,24,1536]{2,1,0:T(8,128)(2,1)} %bitcast.20), calls=%async_computation | async-start | bytes 4718592 | tf_op jit(solution)/shard_map/all_to_all | solution.py:314
  12.0 2.8 %pack.3 = bf16[4,8,24,1536]{3,2,1,0:T(8,128)(2,1)} custom-call(bf16[8,24,3072]{2,1,0:T(8,128)(2,1)} %bitcast.22, bf16[8,24,3072]{2,1,0:T(8,128)(2,1)} %bitcast.24, bf16[8,24,3072]{2,1,0:T(8,128)(2,1)} %bitcast.26, bf16[8,24,3072]{2,1,0:T(8,128)(2,1)} %bitcast.28), custom_call_target="tpu_custom_call" | custom-call | tf_op jit(solution)/shard_map/pack/pallas_call | solution.py:78
  14.8 28.0 %all-to-all-done = bf16[32,24,1536]{2,1,0:T(8,128)(2,1)S(1)} async-done(((bf16[32,24,1536]{2,1,0:T(8,128)(2,1)}), bf16[32,24,1536]{2,1,0:T(8,128)(2,1)S(1)}, u32[]{:S(2)}, u32[]{:S(2)}) %all-to-all-start) | async-done | bytes 2359328 | tf_op jit(solution)/shard_map/all_to_all | solution.py:314
  46.2 7.4 %all-to-all-start.1 = ((bf16[32,24,1536]{2,1,0:T(8,128)(2,1)}), bf16[32,24,1536]{2,1,0:T(8,128)(2,1)}, u32[]{:S(2)}, u32[]{:S(2)}) async-start(bf16[32,24,1536]{2,1,0:T(8,128)(2,1)} %bitcast.19), calls=%async_computation.1 | async-start | bytes 4718592 | tf_op jit(solution)/shard_map/all_to_all | solution.py:314
  53.6 3.7 %collective-permute-start.3 = (bf16[576,768]{1,0:T(8,128)(2,1)}, bf16[576,768]{1,0:T(8,128)(2,1)}, u32[]{:S(2)}, u32[]{:S(2)}) collective-permute-start(bf16[576,768]{1,0:T(8,128)(2,1)} %get-tuple-element.60), channel_id=1, source_target_pairs={{0,224},{32,0},{64,32},{96,64},{128,96},{160,128},{192,160},{224,1... | collective-permute-start | bytes 2654216 | tf_op jit(solution)/shard_map/ppermute | solution.py:310
  57.3 10.2 %collective-permute-done.hk.hv = bf16[576,768]{1,0:T(8,128)(2,1)S(1)} collective-permute-done((bf16[576,768]{1,0:T(8,128)(2,1)S(1)}, bf16[576,768]{1,0:T(8,128)(2,1)S(1)}, u32[]{:S(2)}, u32[]{:S(2)}) %collective-permute-start) | collective-permute-done | bytes 884768 | tf_op jit(solution)/shard_map/ppermute | solution.py:310
  68.5 10.5 %own_pass.2 = (f32[3,768,128]{2,1,0:T(8,128)}, f32[3,768,128]{2,1,0:T(8,128)}, f32[3,8,192]{2,1,0:T(8,128)}, bf16[192,384]{1,0:T(8,128)(2,1)}, bf16[192,384]{1,0...) custom-call(s32[1]{0:T(128)} %bitcast.place, bf16[768,1536]{1,0:T(8,128)(2,1)} %bitcast.13, ...), custom_call_target="tpu_custom_call" | custom-call | flops 199999995904 | bytes 1000 | tf_op jit(solution)/shard_map/own_pass/pallas_call | solution.py:143
  80.3 2.1 %collective-permute-done.1.stats = f32[3,8,192]{2,1,0:T(8,128)S(1)} collective-permute-done((f32[3,8,192]{2,1,0:T(8,128)}, f32[3,8,192]{2,1,0:T(8,128)S(1)}, u32[]{:S(2)}, u32[]{:S(2)}) %collective-permute-start.1) | collective-permute-done | bytes 18464 | tf_op jit(solution)/shard_map/ppermute | solution.py:310
  82.4 2.1 %all-to-all-done.1 = bf16[32,24,1536]{2,1,0:T(8,128)(2,1)} async-done(((bf16[32,24,1536]{2,1,0:T(8,128)(2,1)}), bf16[32,24,1536]{2,1,0:T(8,128)(2,1)}, u32[]{:S(2)}, u32[]{:S(2)}) %all-to-all-start.1) | async-done | bytes 2359328 | tf_op jit(solution)/shard_map/all_to_all | solution.py:314
  86.3 1.7 %collective-permute-start.2 = (bf16[576,768]{1,0:T(8,128)(2,1)S(1)}, bf16[576,768]{1,0:T(8,128)(2,1)S(1)}, u32[]{:S(2)}, u32[]{:S(2)}) collective-permute-start(bf16[576,768]{1,0:T(8,128)(2,1)S(1)} %get-tuple-element.59), channel_id=1, source_target_pairs={{0,32},{32,64},{64,96},{96,128},{128,160},{160,192},{192,224},{224... | collective-permute-start | bytes 2654216 | tf_op jit(solution)/shard_map/ppermute | solution.py:310
  88.0 2.1 %collective-permute-start.7 = (bf16[576,768]{1,0:T(8,128)(2,1)S(1)}, bf16[576,768]{1,0:T(8,128)(2,1)S(1)}, u32[]{:S(2)}, u32[]{:S(2)}) collective-permute-start(bf16[576,768]{1,0:T(8,128)(2,1)S(1)} %get-tuple-element.73), channel_id=1, source_target_pairs={{0,224},{32,0},{64,32},{96,64},{128,96},{160,128},{192,160},{224,1... | collective-permute-start | bytes 2654216 | tf_op jit(solution)/shard_map/ppermute | solution.py:310
  90.1 3.0 %collective-permute-start.4 = (bf16[192,384]{1,0:T(8,128)(2,1)}, bf16[192,384]{1,0:T(8,128)(2,1)S(1)}, u32[]{:S(2)}, u32[]{:S(2)}) collective-permute-start(bf16[192,384]{1,0:T(8,128)(2,1)} %get-tuple-element.66), channel_id=1, source_target_pairs={{0,8},{8,0},{16,24},{24,16},{1,9},{9,1},{17,25},{25,17},{2,10},{10... | collective-permute-start | bytes 442376 | tf_op jit(solution)/shard_map/ppermute | solution.py:319
  93.1 5.4 %later_pass.2 = (bf16[2,192,384]{2,1,0:T(8,128)(2,1)}, bf16[2,192,384]{2,1,0:T(8,128)(2,1)}, bf16[2,192,384]{2,1,0:T(8,128)(2,1)}, bf16[2,192,384]{2,1,0:T(8,128)(2,1)}) custom-call(s32[1]{0:T(128)} %bitcast.place, bf16[768,1536]{1,0:T(8,128)(2,1)} %bitcast.17, bf16[768,1536]{1,0:T(8,128)(2,1)} %bitcast.18, bf16[576,768]{1,0:T(8,128)(2,1)} %collective-permute-done.3.hq.hg, ...), custom_call_target="tpu_custom_call" | custom-call | flops 1000 | bytes 1000 | tf_op jit(solution)/shard_map/later_pass/pallas_call | solution.py:202
  98.6 1.8 %collective-permute-start.6 = (bf16[192,384]{1,0:T(8,128)(2,1)S(1)}, bf16[192,384]{1,0:T(8,128)(2,1)S(1)}, u32[]{:S(2)}, u32[]{:S(2)}) collective-permute-start(bf16[192,384]{1,0:T(8,128)(2,1)S(1)} %copy-done.5), channel_id=1, source_target_pairs={{0,24},{8,16},{16,8},{24,0},{1,25},{9,17},{17,9},{25,1},{2,26},{10... | collective-permute-start | bytes 442376 | tf_op jit(solution)/shard_map/ppermute | solution.py:319
  100.5 4.7 %collective-permute-done.6.refs_3_ = bf16[192,384]{1,0:T(8,128)(2,1)S(1)} collective-permute-done((bf16[192,384]{1,0:T(8,128)(2,1)S(1)}, bf16[192,384]{1,0:T(8,128)(2,1)S(1)}, u32[]{:S(2)}, u32[]{:S(2)}) %collective-permute-start.6) | collective-permute-done | bytes 147488 | tf_op jit(solution)/shard_map/ppermute | solution.py:319
  107.3 9.8 %own_pass.3 = (f32[3,768,128]{2,1,0:T(8,128)S(1)}, f32[3,768,128]{2,1,0:T(8,128)S(1)}, f32[3,8,192]{2,1,0:T(8,128)S(1)}, bf16[192,384]{1,0:T(8,128)(2,1)S(1)}, b...) custom-call(s32[1]{0:T(128)} %bitcast.place, ...), custom_call_target="tpu_custom_call" | custom-call | flops 1000 | bytes 1000 | tf_op jit(solution)/shard_map/own_pass/pallas_call | solution.py:143
  117.1 1.8 %collective-permute-start.8 = (f32[3,8,192]{2,1,0:T(8,128)S(1)}, f32[3,8,192]{2,1,0:T(8,128)S(1)}, u32[]{:S(2)}, u32[]{:S(2)}) collective-permute-start(f32[3,8,192]{2,1,0:T(8,128)S(1)} %get-tuple-element.75), channel_id=1, source_target_pairs={{0,224},{32,0},{64,32},{96,64},{128,96},{160,128},{192,160},{224,1... | collective-permute-start | bytes 55304 | tf_op jit(solution)/shard_map/ppermute | solution.py:310
  118.9 3.6 %collective-permute-start.12 = (bf16[192,384]{1,0:T(8,128)(2,1)S(1)}, bf16[192,384]{1,0:T(8,128)(2,1)S(1)}, u32[]{:S(2)}, u32[]{:S(2)}) collective-permute-start(bf16[192,384]{1,0:T(8,128)(2,1)S(1)} %get-tuple-element.87), channel_id=1, source_target_pairs={{0,8},{8,0},{16,24},{24,16},{1,9},{9,1},{17,25},{25,17},{2,10},{10... | collective-permute-start | bytes 442376 | tf_op jit(solution)/shard_map/ppermute | solution.py:319
  124.8 4.0 %later_pass.3 = (bf16[2,192,384]{2,1,0:T(8,128)(2,1)S(1)}, bf16[2,192,384]{2,1,0:T(8,128)(2,1)S(1)}, bf16[2,192,384]{2,1,0:T(8,128)(2,1)S(1)}, bf16[2,192,384]{2,1,0:T(8,128)(2,1)S(1)}) custom-call(s32[1]{0:T(128)} %bitcast.place, bf16[768,1536]{1,0:T(8,128)(2,1)} %bitcast.8.rows.q.k.v.g, bf16[768,1536]{1,0:T(8,128)(2,1)} %bitcast.8.rows.q.k.v.g, ...), custom_call_target="tpu_custom_call" | custom-call | flops 1000 | bytes 1000 | tf_op jit(solution)/shard_map/later_pass/pallas_call | solution.py:202
  128.8 2.5 %collective-permute-done.14.refs_11_ = bf16[192,384]{1,0:T(8,128)(2,1)S(1)} collective-permute-done((bf16[192,384]{1,0:T(8,128)(2,1)S(1)}, bf16[192,384]{1,0:T(8,128)(2,1)S(1)}, u32[]{:S(2)}, u32[]{:S(2)}) %collective-permute-start.14) | collective-permute-done | bytes 147488 | tf_op jit(solution)/shard_map/ppermute | solution.py:319
  133.4 6.4 %collective-permute-done.16.refs_14_ = bf16[2,192,384]{2,1,0:T(8,128)(2,1)S(1)} collective-permute-done((bf16[2,192,384]{2,1,0:T(8,128)(2,1)S(1)}, bf16[2,192,384]{2,1,0:T(8,128)(2,1)S(1)}, u32[]{:S(2)}, u32[]{:S(2)}) %collective-permute-start.16) | collective-permute-done | bytes 294944 | tf_op jit(solution)/shard_map/ppermute | solution.py:319
  139.8 6.7 %collective-permute-done.17.refs_15_ = bf16[2,192,384]{2,1,0:T(8,128)(2,1)S(1)} collective-permute-done((bf16[2,192,384]{2,1,0:T(8,128)(2,1)S(1)}, bf16[2,192,384]{2,1,0:T(8,128)(2,1)S(1)}, u32[]{:S(2)}, u32[]{:S(2)}) %collective-permute-start.17) | collective-permute-done | bytes 294944 | tf_op jit(solution)/shard_map/ppermute | solution.py:319
  146.5 2.7 %unpack.1 = (bf16[192,3072]{1,0:T(8,128)(2,1)}, bf16[192,3072]{1,0:T(8,128)(2,1)}, bf16[192,3072]{1,0:T(8,128)(2,1)}) custom-call(s32[1]{0:T(128)} %bitcast.place, bf16[192,384]{1,0:T(8,128)(2,1)S(1)} %copy-done.2, bf16[192,384]{1,0:T(8,128)(2,1)S(1)} %collective-permute-done.4.refs_1_, bf16[192,384]{1,0:T(8,128)(2,1)S(1)} %collective-permute-done.5.refs_2_, ...), custom_call_target="tpu_custom_call" | custom-call | tf_op jit(solution)/shard_map/unpack/pallas_call | solution.py:262
  (39 shorter events, 14.0 us)
Async XLA Ops:
  3.4 39.5 %all-to-all-start = ((bf16[32,24,1536]{2,1,0:T(8,128)(2,1)}), bf16[32,24,1536]{2,1,0:T(8,128)(2,1)S(1)}, u32[]{:S(2)}, u32[]{:S(2)}) async-start(bf16[32,24,1536]{2,1,0:T(8,128)(2,1)} %bitcast.20), calls=%async_computation | async-start | bytes 4718592 | tf_op jit(solution)/shard_map/all_to_all | solution.py:314
  44.6 23.0 %collective-permute-start = (bf16[576,768]{1,0:T(8,128)(2,1)S(1)}, bf16[576,768]{1,0:T(8,128)(2,1)S(1)}, u32[]{:S(2)}, u32[]{:S(2)}) collective-permute-start(bf16[576,768]{1,0:T(8,128)(2,1)S(1)} %get-tuple-element.56), channel_id=1, source_target_pairs={{0,32},{32,64},{64,96},{96,128},{128,160},{160,192},{192,224},{224... | collective-permute-start | bytes 2654216 | tf_op jit(solution)/shard_map/ppermute | solution.py:310
  46.2 38.3 %all-to-all-start.1 = ((bf16[32,24,1536]{2,1,0:T(8,128)(2,1)}), bf16[32,24,1536]{2,1,0:T(8,128)(2,1)}, u32[]{:S(2)}, u32[]{:S(2)}) async-start(bf16[32,24,1536]{2,1,0:T(8,128)(2,1)} %bitcast.19), calls=%async_computation.1 | async-start | bytes 4718592 | tf_op jit(solution)/shard_map/all_to_all | solution.py:314
  53.6 39.4 %collective-permute-start.3 = (bf16[576,768]{1,0:T(8,128)(2,1)}, bf16[576,768]{1,0:T(8,128)(2,1)}, u32[]{:S(2)}, u32[]{:S(2)}) collective-permute-start(bf16[576,768]{1,0:T(8,128)(2,1)} %get-tuple-element.60), channel_id=1, source_target_pairs={{0,224},{32,0},{64,32},{96,64},{128,96},{160,128},{192,160},{224,1... | collective-permute-start | bytes 2654216 | tf_op jit(solution)/shard_map/ppermute | solution.py:310
  79.0 3.4 %collective-permute-start.1 = (f32[3,8,192]{2,1,0:T(8,128)}, f32[3,8,192]{2,1,0:T(8,128)S(1)}, u32[]{:S(2)}, u32[]{:S(2)}) collective-permute-start(f32[3,8,192]{2,1,0:T(8,128)} %get-tuple-element.57), channel_id=1, source_target_pairs={{0,224},{32,0},{64,32},{96,64},{128,96},{160,128},{192,160},{224,1... | collective-permute-start | bytes 55304 | tf_op jit(solution)/shard_map/ppermute | solution.py:310
  84.6 8.5 %copy-start.6 = (bf16[192,384]{1,0:T(8,128)(2,1)S(1)}, bf16[192,384]{1,0:T(8,128)(2,1)}, u32[]{:S(2)}) copy-start(bf16[192,384]{1,0:T(8,128)(2,1)} %get-tuple-element.67) | copy-start | bytes 442372
  86.3 21.0 %collective-permute-start.2 = (bf16[576,768]{1,0:T(8,128)(2,1)S(1)}, bf16[576,768]{1,0:T(8,128)(2,1)S(1)}, u32[]{:S(2)}, u32[]{:S(2)}) collective-permute-start(bf16[576,768]{1,0:T(8,128)(2,1)S(1)} %get-tuple-element.59), channel_id=1, source_target_pairs={{0,32},{32,64},{64,96},{96,128},{128,160},{160,192},{192,224},{224... | collective-permute-start | bytes 2654216 | tf_op jit(solution)/shard_map/ppermute | solution.py:310
  88.0 34.5 %collective-permute-start.7 = (bf16[576,768]{1,0:T(8,128)(2,1)S(1)}, bf16[576,768]{1,0:T(8,128)(2,1)S(1)}, u32[]{:S(2)}, u32[]{:S(2)}) collective-permute-start(bf16[576,768]{1,0:T(8,128)(2,1)S(1)} %get-tuple-element.73), channel_id=1, source_target_pairs={{0,224},{32,0},{64,32},{96,64},{128,96},{160,128},{192,160},{224,1... | collective-permute-start | bytes 2654216 | tf_op jit(solution)/shard_map/ppermute | solution.py:310
  90.1 8.5 %collective-permute-start.4 = (bf16[192,384]{1,0:T(8,128)(2,1)}, bf16[192,384]{1,0:T(8,128)(2,1)S(1)}, u32[]{:S(2)}, u32[]{:S(2)}) collective-permute-start(bf16[192,384]{1,0:T(8,128)(2,1)} %get-tuple-element.66), channel_id=1, source_target_pairs={{0,8},{8,0},{16,24},{24,16},{1,9},{9,1},{17,25},{25,17},{2,10},{10... | collective-permute-start | bytes 442376 | tf_op jit(solution)/shard_map/ppermute | solution.py:319
  93.0 7.4 %collective-permute-start.5 = (bf16[192,384]{1,0:T(8,128)(2,1)S(1)}, bf16[192,384]{1,0:T(8,128)(2,1)S(1)}, u32[]{:S(2)}, u32[]{:S(2)}) collective-permute-start(bf16[192,384]{1,0:T(8,128)(2,1)S(1)} %copy-done.6), channel_id=1, source_target_pairs={{0,16},{8,24},{16,0},{24,8},{1,17},{9,25},{17,1},{25,9},{2,18},{10... | collective-permute-start | bytes 442376 | tf_op jit(solution)/shard_map/ppermute | solution.py:319
  93.0 5.5 %copy-start.5 = (bf16[192,384]{1,0:T(8,128)(2,1)S(1)}, bf16[192,384]{1,0:T(8,128)(2,1)}, u32[]{:S(2)}) copy-start(bf16[192,384]{1,0:T(8,128)(2,1)} %get-tuple-element.68) | copy-start | bytes 442372
  98.5 20.4 %collective-permute-start.9 = (bf16[2,192,384]{2,1,0:T(8,128)(2,1)}, bf16[2,192,384]{2,1,0:T(8,128)(2,1)S(1)}, u32[]{:S(2)}, u32[]{:S(2)}) collective-permute-start(bf16[2,192,384]{2,1,0:T(8,128)(2,1)} %get-tuple-element.83), channel_id=1, source_target_pairs={{0,8},{8,0},{16,24},{24,16},{1,9},{9,1},{17,25},{25,17},{2,10},{10... | collective-permute-start | bytes 884744 | tf_op jit(solution)/shard_map/ppermute | solution.py:319
  98.6 6.5 %collective-permute-start.6 = (bf16[192,384]{1,0:T(8,128)(2,1)S(1)}, bf16[192,384]{1,0:T(8,128)(2,1)S(1)}, u32[]{:S(2)}, u32[]{:S(2)}) collective-permute-start(bf16[192,384]{1,0:T(8,128)(2,1)S(1)} %copy-done.5), channel_id=1, source_target_pairs={{0,24},{8,16},{16,8},{24,0},{1,25},{9,17},{17,9},{25,1},{2,26},{10... | collective-permute-start | bytes 442376 | tf_op jit(solution)/shard_map/ppermute | solution.py:319
  100.4 28.3 %collective-permute-start.10 = (bf16[2,192,384]{2,1,0:T(8,128)(2,1)}, bf16[2,192,384]{2,1,0:T(8,128)(2,1)S(1)}, u32[]{:S(2)}, u32[]{:S(2)}) collective-permute-start(bf16[2,192,384]{2,1,0:T(8,128)(2,1)} %get-tuple-element.84), channel_id=1, source_target_pairs={{0,16},{8,24},{16,0},{24,8},{1,17},{9,25},{17,1},{25,9},{2,18},{10... | collective-permute-start | bytes 884744 | tf_op jit(solution)/shard_map/ppermute | solution.py:319
  105.1 23.6 %collective-permute-start.11 = (bf16[2,192,384]{2,1,0:T(8,128)(2,1)}, bf16[2,192,384]{2,1,0:T(8,128)(2,1)S(1)}, u32[]{:S(2)}, u32[]{:S(2)}) collective-permute-start(bf16[2,192,384]{2,1,0:T(8,128)(2,1)} %get-tuple-element.85), channel_id=1, source_target_pairs={{0,24},{8,16},{16,8},{24,0},{1,25},{9,17},{17,9},{25,1},{2,26},{10... | collective-permute-start | bytes 884744 | tf_op jit(solution)/shard_map/ppermute | solution.py:319
  117.1 6.0 %collective-permute-start.8 = (f32[3,8,192]{2,1,0:T(8,128)S(1)}, f32[3,8,192]{2,1,0:T(8,128)S(1)}, u32[]{:S(2)}, u32[]{:S(2)}) collective-permute-start(f32[3,8,192]{2,1,0:T(8,128)S(1)} %get-tuple-element.75), channel_id=1, source_target_pairs={{0,224},{32,0},{64,32},{96,64},{128,96},{160,128},{192,160},{224,1... | collective-permute-start | bytes 55304 | tf_op jit(solution)/shard_map/ppermute | solution.py:310
  118.9 9.9 %collective-permute-start.12 = (bf16[192,384]{1,0:T(8,128)(2,1)S(1)}, bf16[192,384]{1,0:T(8,128)(2,1)S(1)}, u32[]{:S(2)}, u32[]{:S(2)}) collective-permute-start(bf16[192,384]{1,0:T(8,128)(2,1)S(1)} %get-tuple-element.87), channel_id=1, source_target_pairs={{0,8},{8,0},{16,24},{24,16},{1,9},{9,1},{17,25},{25,17},{2,10},{10... | collective-permute-start | bytes 442376 | tf_op jit(solution)/shard_map/ppermute | solution.py:319
  122.5 6.3 %collective-permute-start.13 = (bf16[192,384]{1,0:T(8,128)(2,1)S(1)}, bf16[192,384]{1,0:T(8,128)(2,1)S(1)}, u32[]{:S(2)}, u32[]{:S(2)}) collective-permute-start(bf16[192,384]{1,0:T(8,128)(2,1)S(1)} %get-tuple-element.88), channel_id=1, source_target_pairs={{0,16},{8,24},{16,0},{24,8},{1,17},{9,25},{17,1},{25,9},{2,18},{10... | collective-permute-start | bytes 442376 | tf_op jit(solution)/shard_map/ppermute | solution.py:319
  123.1 8.2 %collective-permute-start.14 = (bf16[192,384]{1,0:T(8,128)(2,1)S(1)}, bf16[192,384]{1,0:T(8,128)(2,1)S(1)}, u32[]{:S(2)}, u32[]{:S(2)}) collective-permute-start(bf16[192,384]{1,0:T(8,128)(2,1)S(1)} %get-tuple-element.89), channel_id=1, source_target_pairs={{0,24},{8,16},{16,8},{24,0},{1,25},{9,17},{17,9},{25,1},{2,26},{10... | collective-permute-start | bytes 442376 | tf_op jit(solution)/shard_map/ppermute | solution.py:319
  124.8 21.8 %copy-start.1 = (bf16[2,192,384]{2,1,0:T(8,128)(2,1)S(1)}, bf16[2,192,384]{2,1,0:T(8,128)(2,1)}, u32[]{:S(2)}) copy-start(bf16[2,192,384]{2,1,0:T(8,128)(2,1)} %get-tuple-element.90.refs_4_) | copy-start | bytes 884740
  124.8 21.8 %copy-start.2 = (bf16[192,384]{1,0:T(8,128)(2,1)S(1)}, bf16[192,384]{1,0:T(8,128)(2,1)}, u32[]{:S(2)}) copy-start(bf16[192,384]{1,0:T(8,128)(2,1)} %get-tuple-element.69.refs_0_) | copy-start | bytes 442372
  131.3 2.1 %collective-permute-start.15 = (bf16[2,192,384]{2,1,0:T(8,128)(2,1)S(1)}, bf16[2,192,384]{2,1,0:T(8,128)(2,1)S(1)}, u32[]{:S(2)}, u32[]{:S(2)}) collective-permute-start(bf16[2,192,384]{2,1,0:T(8,128)(2,1)S(1)} %get-tuple-element.99), channel_id=1, source_target_pairs={{0,8},{8,0},{16,24},{24,16},{1,9},{9,1},{17,25},{25,17},{2,10},{10... | collective-permute-start | bytes 884744 | tf_op jit(solution)/shard_map/ppermute | solution.py:319
  131.5 8.3 %collective-permute-start.16 = (bf16[2,192,384]{2,1,0:T(8,128)(2,1)S(1)}, bf16[2,192,384]{2,1,0:T(8,128)(2,1)S(1)}, u32[]{:S(2)}, u32[]{:S(2)}) collective-permute-start(bf16[2,192,384]{2,1,0:T(8,128)(2,1)S(1)} %get-tuple-element.100), channel_id=1, source_target_pairs={{0,16},{8,24},{16,0},{24,8},{1,17},{9,25},{17,1},{25,9},{2,18},{10... | collective-permute-start | bytes 884744 | tf_op jit(solution)/shard_map/ppermute | solution.py:319
  132.0 14.5 %collective-permute-start.17 = (bf16[2,192,384]{2,1,0:T(8,128)(2,1)S(1)}, bf16[2,192,384]{2,1,0:T(8,128)(2,1)S(1)}, u32[]{:S(2)}, u32[]{:S(2)}) collective-permute-start(bf16[2,192,384]{2,1,0:T(8,128)(2,1)S(1)} %get-tuple-element.101), channel_id=1, source_target_pairs={{0,24},{8,16},{16,8},{24,0},{1,25},{9,17},{17,9},{25,1},{2,26},{10... | collective-permute-start | bytes 884744 | tf_op jit(solution)/shard_map/ppermute | solution.py:319
  (3 other events, 6.5 us)

commit v4 on v3

--- a/solution.py
+++ b/solution.py
@@ -341,7 +341,7 @@
 
     kv_one, qg_one = edges(rows_one)
     kv_one, qg_one = to_plane(kv_one, 1), to_plane(qg_one, -1)
-    dk, dv, stats, *dq = own_pass(place, rows_one, kv_one, one, 60, 200_000_000_000)
+    dk, dv, stats, *dq = own_pass(place, rows_one, kv_one, one, 59, 200_000_000_000)
     dq_one = to_slabs(dq)
     stats = to_plane(stats, -1)
     rows_two, stats = tied(rows_two, stats)

time: 150 us -> 150 us (level)
  no operation moved by 1% of the time
where the time goes in v4:
time: 150 us; the launch traced here: 149 us
  waiting for transfers between devices  63.9 us (43%)
  starting transfers between devices  42.2 us (28%)
  Pallas kernels  41.1 us (27%)
    all_to_all x2, waiting for transfers between devices, to_tiles(): lax.all_to_all(packed, ('g', 'tile'), 0, 0, tiled=True).reshape(OWN, -1)  30.2 us
    pallas_call x2, Pallas kernels, own_pass(): pl.pallas_call(own_kernel, grid=(heads,), in_specs=[PLACE, col(2 * heads)...  20.3 us
    ppermute x12, waiting for transfers between devices, to_slabs(): lax.ppermute(block, 'g', [(i, i ^ partner) for i in range(GROUP)])  20.3 us
    all_to_all x2, starting transfers between devices, to_tiles(): lax.all_to_all(packed, ('g', 'tile'), 0, 0, tiled=True).reshape(OWN, -1)  16 us
    ppermute x12, starting transfers between devices, to_slabs(): lax.ppermute(block, 'g', [(i, i ^ partner) for i in range(GROUP)])  13.9 us
    ppermute x6, waiting for transfers between devices, to_plane(): lax.ppermute(block, 'z', [(i, (i + step) % PLANES) for i in range(PLANES)])  13.4 us
    ppermute x6, starting transfers between devices, to_plane(): lax.ppermute(block, 'z', [(i, (i + step) % PLANES) for i in range(PLANES)])  12.3 us
    pallas_call x2, Pallas kernels, later_pass(): pl.pallas_call(later_kernel, grid=(heads,), in_specs=[PLACE, col(0), col(...  9.43 us
  transfers between devices with their start and end apart: 20, of which 9 were waited for; matrix products, arithmetic and copies ran while one was open for 0% of the time, Pallas kernels for 23%

profile of v4, /device:TPU:1, one launch (start us, length us, event | category | flops | bytes accessed | tf_op | source)
XLA Modules:
  0.0 149.4 jit_solution(13427826146115325872)
XLA Ops:
  0.6 2.8 %pack.2 = bf16[4,8,24,1536]{3,2,1,0:T(8,128)(2,1)} custom-call(bf16[8,24,3072]{2,1,0:T(8,128)(2,1)} %bitcast.21, bf16[8,24,3072]{2,1,0:T(8,128)(2,1)} %bitcast.23, bf16[8,24,3072]{2,1,0:T(8,128)(2,1)} %bitcast.25, bf16[8,24,3072]{2,1,0:T(8,128)(2,1)} %bitcast.27), custom_call_target="tpu_custom_call" | custom-call | tf_op jit(solution)/shard_map/pack/pallas_call | solution.py:78
  3.4 8.6 %all-to-all-start = ((bf16[32,24,1536]{2,1,0:T(8,128)(2,1)}), bf16[32,24,1536]{2,1,0:T(8,128)(2,1)S(1)}, u32[]{:S(2)}, u32[]{:S(2)}) async-start(bf16[32,24,1536]{2,1,0:T(8,128)(2,1)} %bitcast.20), calls=%async_computation | async-start | bytes 4718592 | tf_op jit(solution)/shard_map/all_to_all | solution.py:314
  12.0 2.8 %pack.3 = bf16[4,8,24,1536]{3,2,1,0:T(8,128)(2,1)} custom-call(bf16[8,24,3072]{2,1,0:T(8,128)(2,1)} %bitcast.22, bf16[8,24,3072]{2,1,0:T(8,128)(2,1)} %bitcast.24, bf16[8,24,3072]{2,1,0:T(8,128)(2,1)} %bitcast.26, bf16[8,24,3072]{2,1,0:T(8,128)(2,1)} %bitcast.28), custom_call_target="tpu_custom_call" | custom-call | tf_op jit(solution)/shard_map/pack/pallas_call | solution.py:78
  14.8 28.0 %all-to-all-done = bf16[32,24,1536]{2,1,0:T(8,128)(2,1)S(1)} async-done(((bf16[32,24,1536]{2,1,0:T(8,128)(2,1)}), bf16[32,24,1536]{2,1,0:T(8,128)(2,1)S(1)}, u32[]{:S(2)}, u32[]{:S(2)}) %all-to-all-start) | async-done | bytes 2359328 | tf_op jit(solution)/shard_map/all_to_all | solution.py:314
  46.2 7.4 %all-to-all-start.1 = ((bf16[32,24,1536]{2,1,0:T(8,128)(2,1)}), bf16[32,24,1536]{2,1,0:T(8,128)(2,1)}, u32[]{:S(2)}, u32[]{:S(2)}) async-start(bf16[32,24,1536]{2,1,0:T(8,128)(2,1)} %bitcast.19), calls=%async_computation.1 | async-start | bytes 4718592 | tf_op jit(solution)/shard_map/all_to_all | solution.py:314
  53.6 3.7 %collective-permute-start.3 = (bf16[576,768]{1,0:T(8,128)(2,1)}, bf16[576,768]{1,0:T(8,128)(2,1)}, u32[]{:S(2)}, u32[]{:S(2)}) collective-permute-start(bf16[576,768]{1,0:T(8,128)(2,1)} %get-tuple-element.60), channel_id=1, source_target_pairs={{0,224},{32,0},{64,32},{96,64},{128,96},{160,128},{192,160},{224,1... | collective-permute-start | bytes 2654216 | tf_op jit(solution)/shard_map/ppermute | solution.py:310
  57.3 10.2 %collective-permute-done.hk.hv = bf16[576,768]{1,0:T(8,128)(2,1)S(1)} collective-permute-done((bf16[576,768]{1,0:T(8,128)(2,1)S(1)}, bf16[576,768]{1,0:T(8,128)(2,1)S(1)}, u32[]{:S(2)}, u32[]{:S(2)}) %collective-permute-start) | collective-permute-done | bytes 884768 | tf_op jit(solution)/shard_map/ppermute | solution.py:310
  68.5 10.5 %own_pass.2 = (f32[3,768,128]{2,1,0:T(8,128)}, f32[3,768,128]{2,1,0:T(8,128)}, f32[3,8,192]{2,1,0:T(8,128)}, bf16[192,384]{1,0:T(8,128)(2,1)}, bf16[192,384]{1,0...) custom-call(s32[1]{0:T(128)} %bitcast.place, bf16[768,1536]{1,0:T(8,128)(2,1)} %bitcast.13, ...), custom_call_target="tpu_custom_call" | custom-call | flops 199999995904 | bytes 1000 | tf_op jit(solution)/shard_map/own_pass/pallas_call | solution.py:143
  80.3 2.1 %collective-permute-done.1.stats = f32[3,8,192]{2,1,0:T(8,128)S(1)} collective-permute-done((f32[3,8,192]{2,1,0:T(8,128)}, f32[3,8,192]{2,1,0:T(8,128)S(1)}, u32[]{:S(2)}, u32[]{:S(2)}) %collective-permute-start.1) | collective-permute-done | bytes 18464 | tf_op jit(solution)/shard_map/ppermute | solution.py:310
  82.4 2.1 %all-to-all-done.1 = bf16[32,24,1536]{2,1,0:T(8,128)(2,1)} async-done(((bf16[32,24,1536]{2,1,0:T(8,128)(2,1)}), bf16[32,24,1536]{2,1,0:T(8,128)(2,1)}, u32[]{:S(2)}, u32[]{:S(2)}) %all-to-all-start.1) | async-done | bytes 2359328 | tf_op jit(solution)/shard_map/all_to_all | solution.py:314
  86.3 1.7 %collective-permute-start.2 = (bf16[576,768]{1,0:T(8,128)(2,1)S(1)}, bf16[576,768]{1,0:T(8,128)(2,1)S(1)}, u32[]{:S(2)}, u32[]{:S(2)}) collective-permute-start(bf16[576,768]{1,0:T(8,128)(2,1)S(1)} %get-tuple-element.59), channel_id=1, source_target_pairs={{0,32},{32,64},{64,96},{96,128},{128,160},{160,192},{192,224},{224... | collective-permute-start | bytes 2654216 | tf_op jit(solution)/shard_map/ppermute | solution.py:310
  88.0 2.1 %collective-permute-start.7 = (bf16[576,768]{1,0:T(8,128)(2,1)S(1)}, bf16[576,768]{1,0:T(8,128)(2,1)S(1)}, u32[]{:S(2)}, u32[]{:S(2)}) collective-permute-start(bf16[576,768]{1,0:T(8,128)(2,1)S(1)} %get-tuple-element.73), channel_id=1, source_target_pairs={{0,224},{32,0},{64,32},{96,64},{128,96},{160,128},{192,160},{224,1... | collective-permute-start | bytes 2654216 | tf_op jit(solution)/shard_map/ppermute | solution.py:310
  90.1 3.0 %collective-permute-start.4 = (bf16[192,384]{1,0:T(8,128)(2,1)}, bf16[192,384]{1,0:T(8,128)(2,1)S(1)}, u32[]{:S(2)}, u32[]{:S(2)}) collective-permute-start(bf16[192,384]{1,0:T(8,128)(2,1)} %get-tuple-element.66), channel_id=1, source_target_pairs={{0,8},{8,0},{16,24},{24,16},{1,9},{9,1},{17,25},{25,17},{2,10},{10... | collective-permute-start | bytes 442376 | tf_op jit(solution)/shard_map/ppermute | solution.py:319
  93.1 5.4 %later_pass.2 = (bf16[2,192,384]{2,1,0:T(8,128)(2,1)}, bf16[2,192,384]{2,1,0:T(8,128)(2,1)}, bf16[2,192,384]{2,1,0:T(8,128)(2,1)}, bf16[2,192,384]{2,1,0:T(8,128)(2,1)}) custom-call(s32[1]{0:T(128)} %bitcast.place, bf16[768,1536]{1,0:T(8,128)(2,1)} %bitcast.17, bf16[768,1536]{1,0:T(8,128)(2,1)} %bitcast.18, bf16[576,768]{1,0:T(8,128)(2,1)} %collective-permute-done.3.hq.hg, ...), custom_call_target="tpu_custom_call" | custom-call | flops 1000 | bytes 1000 | tf_op jit(solution)/shard_map/later_pass/pallas_call | solution.py:202
  98.6 1.8 %collective-permute-start.6 = (bf16[192,384]{1,0:T(8,128)(2,1)S(1)}, bf16[192,384]{1,0:T(8,128)(2,1)S(1)}, u32[]{:S(2)}, u32[]{:S(2)}) collective-permute-start(bf16[192,384]{1,0:T(8,128)(2,1)S(1)} %copy-done.5), channel_id=1, source_target_pairs={{0,24},{8,16},{16,8},{24,0},{1,25},{9,17},{17,9},{25,1},{2,26},{10... | collective-permute-start | bytes 442376 | tf_op jit(solution)/shard_map/ppermute | solution.py:319
  100.5 4.7 %collective-permute-done.6.refs_3_ = bf16[192,384]{1,0:T(8,128)(2,1)S(1)} collective-permute-done((bf16[192,384]{1,0:T(8,128)(2,1)S(1)}, bf16[192,384]{1,0:T(8,128)(2,1)S(1)}, u32[]{:S(2)}, u32[]{:S(2)}) %collective-permute-start.6) | collective-permute-done | bytes 147488 | tf_op jit(solution)/shard_map/ppermute | solution.py:319
  107.3 9.8 %own_pass.3 = (f32[3,768,128]{2,1,0:T(8,128)S(1)}, f32[3,768,128]{2,1,0:T(8,128)S(1)}, f32[3,8,192]{2,1,0:T(8,128)S(1)}, bf16[192,384]{1,0:T(8,128)(2,1)S(1)}, b...) custom-call(s32[1]{0:T(128)} %bitcast.place, ...), custom_call_target="tpu_custom_call" | custom-call | flops 1000 | bytes 1000 | tf_op jit(solution)/shard_map/own_pass/pallas_call | solution.py:143
  117.1 1.8 %collective-permute-start.8 = (f32[3,8,192]{2,1,0:T(8,128)S(1)}, f32[3,8,192]{2,1,0:T(8,128)S(1)}, u32[]{:S(2)}, u32[]{:S(2)}) collective-permute-start(f32[3,8,192]{2,1,0:T(8,128)S(1)} %get-tuple-element.75), channel_id=1, source_target_pairs={{0,224},{32,0},{64,32},{96,64},{128,96},{160,128},{192,160},{224,1... | collective-permute-start | bytes 55304 | tf_op jit(solution)/shard_map/ppermute | solution.py:310
  118.9 3.6 %collective-permute-start.12 = (bf16[192,384]{1,0:T(8,128)(2,1)S(1)}, bf16[192,384]{1,0:T(8,128)(2,1)S(1)}, u32[]{:S(2)}, u32[]{:S(2)}) collective-permute-start(bf16[192,384]{1,0:T(8,128)(2,1)S(1)} %get-tuple-element.87), channel_id=1, source_target_pairs={{0,8},{8,0},{16,24},{24,16},{1,9},{9,1},{17,25},{25,17},{2,10},{10... | collective-permute-start | bytes 442376 | tf_op jit(solution)/shard_map/ppermute | solution.py:319
  124.8 4.0 %later_pass.3 = (bf16[2,192,384]{2,1,0:T(8,128)(2,1)S(1)}, bf16[2,192,384]{2,1,0:T(8,128)(2,1)S(1)}, bf16[2,192,384]{2,1,0:T(8,128)(2,1)S(1)}, bf16[2,192,384]{2,1,0:T(8,128)(2,1)S(1)}) custom-call(s32[1]{0:T(128)} %bitcast.place, bf16[768,1536]{1,0:T(8,128)(2,1)} %bitcast.8.rows.q.k.v.g, bf16[768,1536]{1,0:T(8,128)(2,1)} %bitcast.8.rows.q.k.v.g, ...), custom_call_target="tpu_custom_call" | custom-call | flops 1000 | bytes 1000 | tf_op jit(solution)/shard_map/later_pass/pallas_call | solution.py:202
  128.8 2.5 %collective-permute-done.14.refs_11_ = bf16[192,384]{1,0:T(8,128)(2,1)S(1)} collective-permute-done((bf16[192,384]{1,0:T(8,128)(2,1)S(1)}, bf16[192,384]{1,0:T(8,128)(2,1)S(1)}, u32[]{:S(2)}, u32[]{:S(2)}) %collective-permute-start.14) | collective-permute-done | bytes 147488 | tf_op jit(solution)/shard_map/ppermute | solution.py:319
  133.4 6.4 %collective-permute-done.16.refs_14_ = bf16[2,192,384]{2,1,0:T(8,128)(2,1)S(1)} collective-permute-done((bf16[2,192,384]{2,1,0:T(8,128)(2,1)S(1)}, bf16[2,192,384]{2,1,0:T(8,128)(2,1)S(1)}, u32[]{:S(2)}, u32[]{:S(2)}) %collective-permute-start.16) | collective-permute-done | bytes 294944 | tf_op jit(solution)/shard_map/ppermute | solution.py:319
  139.8 6.7 %collective-permute-done.17.refs_15_ = bf16[2,192,384]{2,1,0:T(8,128)(2,1)S(1)} collective-permute-done((bf16[2,192,384]{2,1,0:T(8,128)(2,1)S(1)}, bf16[2,192,384]{2,1,0:T(8,128)(2,1)S(1)}, u32[]{:S(2)}, u32[]{:S(2)}) %collective-permute-start.17) | collective-permute-done | bytes 294944 | tf_op jit(solution)/shard_map/ppermute | solution.py:319
  146.5 2.7 %unpack.1 = (bf16[192,3072]{1,0:T(8,128)(2,1)}, bf16[192,3072]{1,0:T(8,128)(2,1)}, bf16[192,3072]{1,0:T(8,128)(2,1)}) custom-call(s32[1]{0:T(128)} %bitcast.place, bf16[192,384]{1,0:T(8,128)(2,1)S(1)} %copy-done.2, bf16[192,384]{1,0:T(8,128)(2,1)S(1)} %collective-permute-done.4.refs_1_, bf16[192,384]{1,0:T(8,128)(2,1)S(1)} %collective-permute-done.5.refs_2_, ...), custom_call_target="tpu_custom_call" | custom-call | tf_op jit(solution)/shard_map/unpack/pallas_call | solution.py:262
  (39 shorter events, 14.0 us)
Async XLA Ops:
  3.4 39.5 %all-to-all-start = ((bf16[32,24,1536]{2,1,0:T(8,128)(2,1)}), bf16[32,24,1536]{2,1,0:T(8,128)(2,1)S(1)}, u32[]{:S(2)}, u32[]{:S(2)}) async-start(bf16[32,24,1536]{2,1,0:T(8,128)(2,1)} %bitcast.20), calls=%async_computation | async-start | bytes 4718592 | tf_op jit(solution)/shard_map/all_to_all | solution.py:314
  44.6 23.0 %collective-permute-start = (bf16[576,768]{1,0:T(8,128)(2,1)S(1)}, bf16[576,768]{1,0:T(8,128)(2,1)S(1)}, u32[]{:S(2)}, u32[]{:S(2)}) collective-permute-start(bf16[576,768]{1,0:T(8,128)(2,1)S(1)} %get-tuple-element.56), channel_id=1, source_target_pairs={{0,32},{32,64},{64,96},{96,128},{128,160},{160,192},{192,224},{224... | collective-permute-start | bytes 2654216 | tf_op jit(solution)/shard_map/ppermute | solution.py:310
  46.2 38.3 %all-to-all-start.1 = ((bf16[32,24,1536]{2,1,0:T(8,128)(2,1)}), bf16[32,24,1536]{2,1,0:T(8,128)(2,1)}, u32[]{:S(2)}, u32[]{:S(2)}) async-start(bf16[32,24,1536]{2,1,0:T(8,128)(2,1)} %bitcast.19), calls=%async_computation.1 | async-start | bytes 4718592 | tf_op jit(solution)/shard_map/all_to_all | solution.py:314
  53.6 39.4 %collective-permute-start.3 = (bf16[576,768]{1,0:T(8,128)(2,1)}, bf16[576,768]{1,0:T(8,128)(2,1)}, u32[]{:S(2)}, u32[]{:S(2)}) collective-permute-start(bf16[576,768]{1,0:T(8,128)(2,1)} %get-tuple-element.60), channel_id=1, source_target_pairs={{0,224},{32,0},{64,32},{96,64},{128,96},{160,128},{192,160},{224,1... | collective-permute-start | bytes 2654216 | tf_op jit(solution)/shard_map/ppermute | solution.py:310
  79.0 3.4 %collective-permute-start.1 = (f32[3,8,192]{2,1,0:T(8,128)}, f32[3,8,192]{2,1,0:T(8,128)S(1)}, u32[]{:S(2)}, u32[]{:S(2)}) collective-permute-start(f32[3,8,192]{2,1,0:T(8,128)} %get-tuple-element.57), channel_id=1, source_target_pairs={{0,224},{32,0},{64,32},{96,64},{128,96},{160,128},{192,160},{224,1... | collective-permute-start | bytes 55304 | tf_op jit(solution)/shard_map/ppermute | solution.py:310
  84.6 8.5 %copy-start.6 = (bf16[192,384]{1,0:T(8,128)(2,1)S(1)}, bf16[192,384]{1,0:T(8,128)(2,1)}, u32[]{:S(2)}) copy-start(bf16[192,384]{1,0:T(8,128)(2,1)} %get-tuple-element.67) | copy-start | bytes 442372
  86.3 21.0 %collective-permute-start.2 = (bf16[576,768]{1,0:T(8,128)(2,1)S(1)}, bf16[576,768]{1,0:T(8,128)(2,1)S(1)}, u32[]{:S(2)}, u32[]{:S(2)}) collective-permute-start(bf16[576,768]{1,0:T(8,128)(2,1)S(1)} %get-tuple-element.59), channel_id=1, source_target_pairs={{0,32},{32,64},{64,96},{96,128},{128,160},{160,192},{192,224},{224... | collective-permute-start | bytes 2654216 | tf_op jit(solution)/shard_map/ppermute | solution.py:310
  88.0 34.5 %collective-permute-start.7 = (bf16[576,768]{1,0:T(8,128)(2,1)S(1)}, bf16[576,768]{1,0:T(8,128)(2,1)S(1)}, u32[]{:S(2)}, u32[]{:S(2)}) collective-permute-start(bf16[576,768]{1,0:T(8,128)(2,1)S(1)} %get-tuple-element.73), channel_id=1, source_target_pairs={{0,224},{32,0},{64,32},{96,64},{128,96},{160,128},{192,160},{224,1... | collective-permute-start | bytes 2654216 | tf_op jit(solution)/shard_map/ppermute | solution.py:310
  90.1 8.5 %collective-permute-start.4 = (bf16[192,384]{1,0:T(8,128)(2,1)}, bf16[192,384]{1,0:T(8,128)(2,1)S(1)}, u32[]{:S(2)}, u32[]{:S(2)}) collective-permute-start(bf16[192,384]{1,0:T(8,128)(2,1)} %get-tuple-element.66), channel_id=1, source_target_pairs={{0,8},{8,0},{16,24},{24,16},{1,9},{9,1},{17,25},{25,17},{2,10},{10... | collective-permute-start | bytes 442376 | tf_op jit(solution)/shard_map/ppermute | solution.py:319
  93.0 7.4 %collective-permute-start.5 = (bf16[192,384]{1,0:T(8,128)(2,1)S(1)}, bf16[192,384]{1,0:T(8,128)(2,1)S(1)}, u32[]{:S(2)}, u32[]{:S(2)}) collective-permute-start(bf16[192,384]{1,0:T(8,128)(2,1)S(1)} %copy-done.6), channel_id=1, source_target_pairs={{0,16},{8,24},{16,0},{24,8},{1,17},{9,25},{17,1},{25,9},{2,18},{10... | collective-permute-start | bytes 442376 | tf_op jit(solution)/shard_map/ppermute | solution.py:319
  93.0 5.5 %copy-start.5 = (bf16[192,384]{1,0:T(8,128)(2,1)S(1)}, bf16[192,384]{1,0:T(8,128)(2,1)}, u32[]{:S(2)}) copy-start(bf16[192,384]{1,0:T(8,128)(2,1)} %get-tuple-element.68) | copy-start | bytes 442372
  98.5 20.4 %collective-permute-start.9 = (bf16[2,192,384]{2,1,0:T(8,128)(2,1)}, bf16[2,192,384]{2,1,0:T(8,128)(2,1)S(1)}, u32[]{:S(2)}, u32[]{:S(2)}) collective-permute-start(bf16[2,192,384]{2,1,0:T(8,128)(2,1)} %get-tuple-element.83), channel_id=1, source_target_pairs={{0,8},{8,0},{16,24},{24,16},{1,9},{9,1},{17,25},{25,17},{2,10},{10... | collective-permute-start | bytes 884744 | tf_op jit(solution)/shard_map/ppermute | solution.py:319
  98.6 6.5 %collective-permute-start.6 = (bf16[192,384]{1,0:T(8,128)(2,1)S(1)}, bf16[192,384]{1,0:T(8,128)(2,1)S(1)}, u32[]{:S(2)}, u32[]{:S(2)}) collective-permute-start(bf16[192,384]{1,0:T(8,128)(2,1)S(1)} %copy-done.5), channel_id=1, source_target_pairs={{0,24},{8,16},{16,8},{24,0},{1,25},{9,17},{17,9},{25,1},{2,26},{10... | collective-permute-start | bytes 442376 | tf_op jit(solution)/shard_map/ppermute | solution.py:319
  100.4 28.3 %collective-permute-start.10 = (bf16[2,192,384]{2,1,0:T(8,128)(2,1)}, bf16[2,192,384]{2,1,0:T(8,128)(2,1)S(1)}, u32[]{:S(2)}, u32[]{:S(2)}) collective-permute-start(bf16[2,192,384]{2,1,0:T(8,128)(2,1)} %get-tuple-element.84), channel_id=1, source_target_pairs={{0,16},{8,24},{16,0},{24,8},{1,17},{9,25},{17,1},{25,9},{2,18},{10... | collective-permute-start | bytes 884744 | tf_op jit(solution)/shard_map/ppermute | solution.py:319
  105.1 23.6 %collective-permute-start.11 = (bf16[2,192,384]{2,1,0:T(8,128)(2,1)}, bf16[2,192,384]{2,1,0:T(8,128)(2,1)S(1)}, u32[]{:S(2)}, u32[]{:S(2)}) collective-permute-start(bf16[2,192,384]{2,1,0:T(8,128)(2,1)} %get-tuple-element.85), channel_id=1, source_target_pairs={{0,24},{8,16},{16,8},{24,0},{1,25},{9,17},{17,9},{25,1},{2,26},{10... | collective-permute-start | bytes 884744 | tf_op jit(solution)/shard_map/ppermute | solution.py:319
  117.1 6.0 %collective-permute-start.8 = (f32[3,8,192]{2,1,0:T(8,128)S(1)}, f32[3,8,192]{2,1,0:T(8,128)S(1)}, u32[]{:S(2)}, u32[]{:S(2)}) collective-permute-start(f32[3,8,192]{2,1,0:T(8,128)S(1)} %get-tuple-element.75), channel_id=1, source_target_pairs={{0,224},{32,0},{64,32},{96,64},{128,96},{160,128},{192,160},{224,1... | collective-permute-start | bytes 55304 | tf_op jit(solution)/shard_map/ppermute | solution.py:310
  118.9 9.9 %collective-permute-start.12 = (bf16[192,384]{1,0:T(8,128)(2,1)S(1)}, bf16[192,384]{1,0:T(8,128)(2,1)S(1)}, u32[]{:S(2)}, u32[]{:S(2)}) collective-permute-start(bf16[192,384]{1,0:T(8,128)(2,1)S(1)} %get-tuple-element.87), channel_id=1, source_target_pairs={{0,8},{8,0},{16,24},{24,16},{1,9},{9,1},{17,25},{25,17},{2,10},{10... | collective-permute-start | bytes 442376 | tf_op jit(solution)/shard_map/ppermute | solution.py:319
  122.5 6.3 %collective-permute-start.13 = (bf16[192,384]{1,0:T(8,128)(2,1)S(1)}, bf16[192,384]{1,0:T(8,128)(2,1)S(1)}, u32[]{:S(2)}, u32[]{:S(2)}) collective-permute-start(bf16[192,384]{1,0:T(8,128)(2,1)S(1)} %get-tuple-element.88), channel_id=1, source_target_pairs={{0,16},{8,24},{16,0},{24,8},{1,17},{9,25},{17,1},{25,9},{2,18},{10... | collective-permute-start | bytes 442376 | tf_op jit(solution)/shard_map/ppermute | solution.py:319
  123.1 8.2 %collective-permute-start.14 = (bf16[192,384]{1,0:T(8,128)(2,1)S(1)}, bf16[192,384]{1,0:T(8,128)(2,1)S(1)}, u32[]{:S(2)}, u32[]{:S(2)}) collective-permute-start(bf16[192,384]{1,0:T(8,128)(2,1)S(1)} %get-tuple-element.89), channel_id=1, source_target_pairs={{0,24},{8,16},{16,8},{24,0},{1,25},{9,17},{17,9},{25,1},{2,26},{10... | collective-permute-start | bytes 442376 | tf_op jit(solution)/shard_map/ppermute | solution.py:319
  124.8 21.8 %copy-start.1 = (bf16[2,192,384]{2,1,0:T(8,128)(2,1)S(1)}, bf16[2,192,384]{2,1,0:T(8,128)(2,1)}, u32[]{:S(2)}) copy-start(bf16[2,192,384]{2,1,0:T(8,128)(2,1)} %get-tuple-element.90.refs_4_) | copy-start | bytes 884740
  124.8 21.8 %copy-start.2 = (bf16[192,384]{1,0:T(8,128)(2,1)S(1)}, bf16[192,384]{1,0:T(8,128)(2,1)}, u32[]{:S(2)}) copy-start(bf16[192,384]{1,0:T(8,128)(2,1)} %get-tuple-element.69.refs_0_) | copy-start | bytes 442372
  131.3 2.1 %collective-permute-start.15 = (bf16[2,192,384]{2,1,0:T(8,128)(2,1)S(1)}, bf16[2,192,384]{2,1,0:T(8,128)(2,1)S(1)}, u32[]{:S(2)}, u32[]{:S(2)}) collective-permute-start(bf16[2,192,384]{2,1,0:T(8,128)(2,1)S(1)} %get-tuple-element.99), channel_id=1, source_target_pairs={{0,8},{8,0},{16,24},{24,16},{1,9},{9,1},{17,25},{25,17},{2,10},{10... | collective-permute-start | bytes 884744 | tf_op jit(solution)/shard_map/ppermute | solution.py:319
  131.5 8.3 %collective-permute-start.16 = (bf16[2,192,384]{2,1,0:T(8,128)(2,1)S(1)}, bf16[2,192,384]{2,1,0:T(8,128)(2,1)S(1)}, u32[]{:S(2)}, u32[]{:S(2)}) collective-permute-start(bf16[2,192,384]{2,1,0:T(8,128)(2,1)S(1)} %get-tuple-element.100), channel_id=1, source_target_pairs={{0,16},{8,24},{16,0},{24,8},{1,17},{9,25},{17,1},{25,9},{2,18},{10... | collective-permute-start | bytes 884744 | tf_op jit(solution)/shard_map/ppermute | solution.py:319
  132.0 14.5 %collective-permute-start.17 = (bf16[2,192,384]{2,1,0:T(8,128)(2,1)S(1)}, bf16[2,192,384]{2,1,0:T(8,128)(2,1)S(1)}, u32[]{:S(2)}, u32[]{:S(2)}) collective-permute-start(bf16[2,192,384]{2,1,0:T(8,128)(2,1)S(1)} %get-tuple-element.101), channel_id=1, source_target_pairs={{0,24},{8,16},{16,8},{24,0},{1,25},{9,17},{17,9},{25,1},{2,26},{10... | collective-permute-start | bytes 884744 | tf_op jit(solution)/shard_map/ppermute | solution.py:319
  (3 other events, 6.5 us)
